TPU v7x, 512 devices: a whole 4x8x8 slice. The times are simulated.
512 devices in a mesh: row: 32 (over z, x), col: 16 (over y, core).
Axes of the slice: x: 4, y: 8, z: 8, core: 2. Of those that a mesh axis runs over, the one named last changes fastest.
Arguments:
- covariance: float32 [16384, 16384], P('row', 'col'), as said below
Outputs:
- factored: float32 [16384, 16384], P('row', 'col')
Inputs may be any that keep to these rules, and one draw needn't show every extreme that they name: covariance is symmetric and positive definite in natural order, with smallest eigenvalue well above zero.
All inputs are finite; a program needn't handle non-finite values.
Results may differ from a plain program's by a relative error of at most 0.0001.
Values sent between devices are 32-bit elements; how exact they have to be, the bound alone decides.
No kernel may reach another device: no remote copies, remote signals or barrier semaphores. Data moves between devices by JAX's collectives and lax.ppermute only.
A program may use at most 64 MiB of HBM per device.

v0:
```python
import jax
import jax.numpy as jnp
from jax import lax
from jax.sharding import PartitionSpec as P

NB = 256
STEPS = 2


def spread(value, axis, source):
    kept = jnp.where(lax.axis_index(axis) == source, value, 0).astype(value.dtype)
    return lax.psum(kept, axis)


def on_device(covariance):
    n_row = lax.axis_size("row")
    n_col = lax.axis_size("col")
    row_count = covariance.shape[0] // NB
    col_count = covariance.shape[1] // NB
    own_row = lax.axis_index("row")
    own_col = lax.axis_index("col")
    row_ids = jnp.repeat(jnp.arange(row_count, dtype=jnp.int32) * n_row + own_row, NB)
    col_ids = jnp.repeat(jnp.arange(col_count, dtype=jnp.int32) * n_col + own_col, NB)
    mirrors = n_row // n_col
    matrix = covariance
    for step in range(STEPS):
        local_col = step // n_col
        local_row = step // n_row
        column = lax.slice_in_dim(matrix, local_col * NB, (local_col + 1) * NB, axis=1)
        corner = lax.slice_in_dim(column, local_row * NB, (local_row + 1) * NB, axis=0)
        corner = spread(corner, "row", step % n_row)
        factor = jnp.linalg.cholesky(corner)
        solved = jax.scipy.linalg.solve_triangular(factor, column.T, lower=True).T
        corner_tiled = jnp.tile(factor, (row_count, 1))
        marks = row_ids[:, None]
        panel = jnp.where(marks > step, solved, jnp.where(marks == step, corner_tiled, 0.0))
        panel_left_rows = spread(panel, "col", step % n_col)
        pieces = []
        for mirror_index in range(mirrors):
            pieces.append(spread(panel_left_rows, "row", own_col + n_col * mirror_index))
        stacked = jnp.stack(pieces)
        panel_left_cols = (
            stacked.reshape(mirrors, row_count, NB, NB)
            .transpose(1, 0, 2, 3)
            .reshape(row_count * mirrors * NB, NB)
        )
        block_cols = matrix
        product = lax.dot_general(
            panel_left_rows,
            panel_left_cols,
            (((1,), (1,)), ((), ())),
            precision=lax.Precision.HIGHEST,
            preferred_element_type=jnp.float32,
        )
        trailing = (row_ids[:, None] > step) & (col_ids[None, :] > step)
        updated = jnp.where(trailing, block_cols - product, block_cols)
        panel_wide = jnp.tile(panel_left_rows, (1, col_count - 0))
        updated = jnp.where(col_ids[None, :] == step, panel_wide, updated)
        updated = jnp.where((row_ids[:, None] == step) & (col_ids[None, :] > step), 0.0, updated)
        matrix = updated
    return matrix


def solution(mesh):
    return jax.shard_map(
        on_device,
        mesh=mesh,
        in_specs=(P("row", "col"),),
        out_specs=P("row", "col"),
        check_vma=False,
    )
```

profile of v0, /device:TPU:16, one launch (start us, length us, event | category | flops | bytes accessed | tf_op | source)
XLA Modules:
  0.0 1029.1 jit_solution(9189841926808365455)
XLA Ops:
  6.5 1.9 copy.12
  9.6 1.1 slice_bitcast_fusion.1
  10.7 160.1 %all-reduce.10.cloned.1.call-done = f32[256,256]{0,1:T(8,128)} async-done(((f32[256,256]{0,1:T(8,128)}), f32[256,256]{0,1:T(8,128)}) %all-reduce.10.cloned.1.call-update) | async-done | bytes 262160 | tf_op jit(solution)/shard_map/psum | solution.py:12
  170.7 1.1 copy.13
  172.8 11.7 %cholesky.130 = f32[128,128]{1,0:T(8,128)S(1)} custom-call(f32[128,128]{1,0:T(8,128)S(1)} %cholesky.194), custom_call_target="Cholesky" | custom-call | tf_op jit(solution)/shard_map/jit(cholesky)/cholesky | solution.py:32
  184.6 9.8 custom-call.13
  194.9 11.7 %cholesky.147 = f32[128,128]{1,0:T(8,128)S(1)} custom-call(f32[128,128]{1,0:T(8,128)S(1)} %convolution_subtract_fusion.3), custom_call_target="Cholesky" | custom-call | tf_op jit(solution)/shard_map/jit(cholesky)/cholesky | solution.py:32
  209.1 4.1 while.4
  209.9 1.3 bitcast_dynamic-update-slice_fusion.4
  211.8 1.3 bitcast_dynamic-update-slice_fusion.4
  213.2 19.7 %custom-call.14 = f32[2,128,128]{1,2,0:T(8,128)S(1)} custom-call(f32[2,128,128]{2,1,0:T(8,128)S(1)} %get-tuple-element.21), custom_call_target="InvertDiagBlocksLowerTriangular" | custom-call | tf_op jit(solution)/shard_map/jit(_solve_triangular)/triangular_solve | solution.py:33
  235.3 109.7 %all-reduce.12.cloned.1.call-done = f32[512,256]{0,1:T(8,128)} async-done(((f32[512,256]{0,1:T(8,128)}), f32[512,256]{0,1:T(8,128)}) %all-reduce.12.cloned.1.call-update) | async-done | bytes 524304 | tf_op jit(solution)/shard_map/psum | solution.py:12
  345.0 1.2 broadcast_select_fusion.2
  346.2 1.0 copy.28
  348.4 164.2 %all-reduce.20.cloned.1.call-done = (f32[1,2,256,256]{3,2,0,1:T(8,128)}, f32[1,2,256,256]{3,2,0,1:T(8,128)}) async-done(((f32[1,2,256,256]{3,2,0,1:T(8,128)}, f32[1,2,256,256]{3,2,0,1:T(8,128)}), (f32[1,2,256,256]{3,2,0,1:T(8,128)}, f32[1,2,256,256]{3,2,0,1:T(8,128)})) %all-reduce.20.cloned.1.call-update) | async-done | bytes 1048592 | tf_op jit(solution)/shard_map/psum | solution.py:12
  512.6 1.3 pad_maximum_fusion
  513.9 3.9 fusion.1
  518.9 152.3 %all-reduce.14.cloned.1.call-done = f32[256,256]{0,1:T(8,128)} async-done(((f32[256,256]{0,1:T(8,128)}), f32[256,256]{0,1:T(8,128)}) %all-reduce.14.cloned.1.call-update) | async-done | bytes 262160 | tf_op jit(solution)/shard_map/psum | solution.py:12
  671.2 1.1 copy.20
  673.2 11.7 %cholesky.164 = f32[128,128]{1,0:T(8,128)S(1)} custom-call(f32[128,128]{1,0:T(8,128)S(1)} %cholesky.197), custom_call_target="Cholesky" | custom-call | tf_op jit(solution)/shard_map/jit(cholesky)/cholesky | solution.py:32
  685.0 9.8 custom-call.15
  695.3 11.7 %cholesky.181 = f32[128,128]{1,0:T(8,128)S(1)} custom-call(f32[128,128]{1,0:T(8,128)S(1)} %convolution_subtract_fusion.2), custom_call_target="Cholesky" | custom-call | tf_op jit(solution)/shard_map/jit(cholesky)/cholesky | solution.py:32
  710.1 4.1 while.5
  710.9 1.3 bitcast_dynamic-update-slice_fusion.5
  712.9 1.3 bitcast_dynamic-update-slice_fusion.5
  714.9 20.5 %custom-call.16 = f32[2,128,128]{1,2,0:T(8,128)S(1)} custom-call(f32[2,128,128]{2,1,0:T(8,128)} %copy-done.3), custom_call_target="InvertDiagBlocksLowerTriangular" | custom-call | tf_op jit(solution)/shard_map/jit(_solve_triangular)/triangular_solve | solution.py:33
  737.6 109.7 %all-reduce.16.cloned.1.call-done = f32[512,256]{0,1:T(8,128)} async-done(((f32[512,256]{0,1:T(8,128)}), f32[512,256]{0,1:T(8,128)}) %all-reduce.16.cloned.1.call-update) | async-done | bytes 524304 | tf_op jit(solution)/shard_map/psum | solution.py:12
  847.3 1.2 broadcast_select_fusion.3
  850.7 163.7 %all-reduce.18.cloned.1.call-done = (f32[1,2,256,256]{3,2,0,1:T(8,128)}, f32[1,2,256,256]{3,2,0,1:T(8,128)}) async-done(((f32[1,2,256,256]{3,2,0,1:T(8,128)}, f32[1,2,256,256]{3,2,0,1:T(8,128)}), (f32[1,2,256,256]{3,2,0,1:T(8,128)}, f32[1,2,256,256]{3,2,0,1:T(8,128)})) %all-reduce.18.cloned.1.call-update) | async-done | bytes 1048592 | tf_op jit(solution)/shard_map/psum | solution.py:12
  1014.4 1.3 pad_maximum_fusion.1
  1015.7 3.7 fusion.3
  1019.4 2.9 copy.25
  (91 shorter events, 19.1 us)
Async XLA Ops:
  6.5 164.2 %all-reduce.10.cloned.1.call-start = ((), (), s32[]{:S(2)}) async-start(), calls=%async_computation | async-start | bytes 524288 | tf_op jit(solution)/shard_map/psum | solution.py:12
  8.5 186.4 %copy-start = (f32[512,1024]{0,1:T(8,128)}, f32[512,1024]{0,1:T(8,128)S(1)}, u32[]{:S(2)}) copy-start(f32[512,1024]{0,1:T(8,128)S(1)} %copy.12) | copy-start | bytes 6291460
  9.3 335.6 %all-reduce.12.cloned.1.call-start = ((), (), s32[]{:S(2)}) async-start(), calls=%async_computation.1 | async-start | bytes 1048576 | tf_op jit(solution)/shard_map/psum | solution.py:12
  235.2 277.4 %all-reduce.20.cloned.1.call-start = ((), (), s32[]{:S(2)}) async-start(), calls=%async_computation.5 | async-start | bytes 2097152 | tf_op jit(solution)/shard_map/psum | solution.py:12
  347.2 166.8 %copy-start.1 = (f32[512,256]{0,1:T(8,128)S(1)}, f32[512,256]{0,1:T(8,128)}, u32[]{:S(2)}) copy-start(f32[512,256]{0,1:T(8,128)} %all-reduce.12.cloned.1.call-done) | copy-start | bytes 1572868
  348.2 323.0 %all-reduce.14.cloned.1.call-start = ((), (), s32[]{:S(2)}) async-start(), calls=%async_computation.2 | async-start | bytes 524288 | tf_op jit(solution)/shard_map/psum | solution.py:12
  518.6 328.7 %all-reduce.16.cloned.1.call-start = ((), (), s32[]{:S(2)}) async-start(), calls=%async_computation.3 | async-start | bytes 1048576 | tf_op jit(solution)/shard_map/psum | solution.py:12
  714.2 0.7 copy-start.3
  737.5 276.9 %all-reduce.18.cloned.1.call-start = ((), (), s32[]{:S(2)}) async-start(), calls=%async_computation.4 | async-start | bytes 2097152 | tf_op jit(solution)/shard_map/psum | solution.py:12
  849.5 166.2 %copy-start.2 = (f32[512,256]{0,1:T(8,128)S(1)}, f32[512,256]{0,1:T(8,128)}, u32[]{:S(2)}) copy-start(f32[512,256]{0,1:T(8,128)} %all-reduce.16.cloned.1.call-done) | copy-start | bytes 1572868
Sparse Core Ops, SparseCore 0:
  10.8 159.8 all-reduce.9
  235.3 109.5 all-reduce.11
  348.9 163.6 all-reduce.19
  518.7 152.4 all-reduce.13
  737.6 109.5 all-reduce.15
  850.7 163.6 all-reduce.17
where the time goes:
time: 1030 us
  waiting for transfers between devices  860 us (83%)
  other arithmetic  119 us (12%)
  local copies, waits for them, and re-layouts  22 us (2%)
  between operations  16.4 us (2%)
  matrix products  11.2 us (1%)
    psum x6, waiting for transfers between devices, spread(): return lax.psum(kept, axis)  860 us
    another operation x13, other arithmetic, on_device(): factor = jnp.linalg.cholesky(corner)  68.6 us
    another operation x5, other arithmetic, on_device(): solved = jax.scipy.linalg.solve_triangular(factor, column.T, lower=True).T  40.2 us
  transfers between devices with their start and end apart: 6, of which 6 were waited for; matrix products, arithmetic and copies ran while one was open for 0% of the time, Pallas kernels for 0%

commit v1 on v0

v1 whole, which is shorter than its diff:
```python
import functools

import jax
import jax.numpy as jnp
import numpy as np
from jax import lax
from jax.experimental import pallas as pl
from jax.experimental.pallas import tpu as pltpu
from jax.sharding import PartitionSpec as P

NB = 256
PANEL = 512
NZ, NX, NY, NK = 8, 4, 8, 2
B = 128
S = 8
F32 = jnp.float32
BOTH = ("row", "col")


def dot(a, b, dims):
    return lax.dot_general(a, b, (dims, ((), ())), precision=lax.Precision.HIGHEST, preferred_element_type=F32)


def device(z, x, y, k):
    return (((z % NZ) * NX + x % NX) * NY + y % NY) * NK + k


DEVICES = [(z, x, y, k) for z in range(NZ) for x in range(NX) for y in range(NY) for k in range(NK)]


def send(value, target):
    pairs = []
    for at in DEVICES:
        to = target(*at)
        if to is not None:
            pairs.append((device(*at), device(*to)))
    return lax.ppermute(value, BOTH, pairs)


HOPS = [({0: 3}, {0: 5}), ({0: 1, 3: 4, 5: 6}, {0: 7, 3: 2})]


def along_y(part, where=lambda z, x, k: True):
    return lambda z, x, y, k: (z, x, part[y], k) if y in part and where(z, x, k) else None


def along_z(part, where=lambda x, y, k: True):
    return lambda z, x, y, k: (part[z], x, y, k) if z in part and where(x, y, k) else None


def pair_x(where):
    other = {0: 3, 1: 2}
    return lambda z, x, y, k: (z, other[x], y, k) if x in other and where(z, y, k) else None


def either(first, second):
    def target(z, x, y, k):
        return (second if k else first)(z, x, y, k)

    return target


def nowhere(z, x, y, k):
    return None


def spread_corner(block, row, col):
    core = col
    blocks = [block[:B, :B], block[B:, :B], block[B:, B:]]
    diagonal = row == core
    half = [jnp.where(core == 0, blocks[0], blocks[1]), jnp.where(core == 0, blocks[1], blocks[2]), blocks[2]]
    mine = jnp.concatenate([jnp.where(diagonal, t, h) for t, h in zip(blocks, half)])
    theirs = send(mine, lambda z, x, y, k: (z, 1 - x, y, k) if z == 0 and x < 2 and y == 0 else None)
    piece = jnp.concatenate([jnp.where(diagonal, mine, theirs), jnp.where(diagonal, theirs, mine)[: 2 * B]])
    piece = jnp.where((row < 2) & (col < 2), piece, 0.0)
    left = lambda z, x, k: z == 0 and x < 2
    rounds = [
        [(along_y(HOPS[0][s], left), along_z(HOPS[0][s], lambda x, y, k: x < 2 and y == 0)) for s in (0, 1)],
        [(along_y(HOPS[1][s], left), along_z(HOPS[1][s], lambda x, y, k: x < 2 and y == 0)) for s in (0, 1)],
        [
            (along_z(HOPS[0][0], lambda x, y, k: x < 2), pair_x(lambda z, y, k: y == 0)),
            (along_z(HOPS[0][1], lambda x, y, k: x < 2), nowhere),
        ],
        [(along_z(HOPS[1][s], lambda x, y, k: x < 2), along_y(HOPS[0][s])) for s in (0, 1)],
        [
            (pair_x(lambda z, y, k: True), along_y(HOPS[1][0])),
            (nowhere, along_y(HOPS[1][1])),
        ],
    ]
    for steps in rounds:
        got = [send(piece, either(*step)) for step in steps]
        piece = piece + got[0] + got[1]
    other = send(piece, lambda z, x, y, k: (z, x, y, 1 - k))
    return piece, other


def spread_rows(top):
    half = top.shape[1] // 2
    x_index = lax.axis_index("row") % NX
    far = send(top[:, half:], pair_x(lambda z, y, k: z == 0))
    quarter = jnp.where(x_index < 2, top[:, :half], far)
    quarter = jnp.where(lax.axis_index("row") < NX, quarter, 0.0)
    for hops in HOPS:
        got = [send(quarter, along_z(hop)) for hop in hops]
        quarter = quarter + got[0] + got[1]
    behind = send(quarter, lambda z, x, y, k: (z, x + 1, y, k))
    ahead = send(quarter, lambda z, x, y, k: (z, x - 1, y, k))
    low = send(behind[: NB // 2], lambda z, x, y, k: (z, x + 1, y, k))
    high = send(ahead[NB // 2 :], lambda z, x, y, k: (z, x - 1, y, k))
    return quarter, behind, ahead, low, high


def spread_cols(left):
    left = jnp.where(lax.axis_index("col") < NK, left, 0.0)
    for hops in HOPS:
        got = [send(left, along_y(hop)) for hop in hops]
        left = left + got[0] + got[1]
    other = send(left, lambda z, x, y, k: (z, x, y, 1 - k))
    return left, other


def factor_block(d, up, inv):
    lane = lax.broadcasted_iota(jnp.int32, (S, B), 1)
    sub = lax.broadcasted_iota(jnp.int32, (S, B), 0)

    def stack(rows):
        out = rows[0]
        for i in range(1, S):
            out = jnp.where(sub == i, rows[i], out)
        return out

    for k in range(0, B, S):
        here = (lane >= k) & (lane < k + S)
        p = [jnp.broadcast_to(d[k + i : k + i + 1, :], (S, B)) for i in range(S)]
        s = {(i, j): jnp.broadcast_to(p[i][:, k + j : k + j + 1], (S, B)) for i in range(S) for j in range(i + 1)}
        r, w = [], {}
        for j in range(S):
            r.append(lax.rsqrt(s[j, j]))
            for i in range(j + 1, S):
                s[i, j] = s[i, j] * r[j]
            for i in range(j + 1, S):
                for m in range(j + 1, i + 1):
                    s[i, m] = s[i, m] - s[i, j] * s[m, j]
            w[j, j] = r[j]
            for m in range(j):
                acc = s[j, m] * w[m, m]
                for q in range(m + 1, j):
                    acc = acc + s[j, q] * w[q, m]
                w[j, m] = -r[j] * acc
        q = [jnp.where(here, jnp.where(lane == k + i, 1.0, 0.0), p[i]) for i in range(S)]
        u, t = [], []
        for i in range(S):
            a = w[i, 0] * q[0]
            b = w[i, 0] * p[0]
            for m in range(1, i + 1):
                a = a + w[i, m] * q[m]
                b = b + w[i, m] * p[m]
            u.append(a)
            t.append(b)
        up[k : k + S, :] = jnp.where(lane >= k + sub, stack(t), 0.0)
        inv[k : k + S, :] = jnp.where(lane <= k + sub, stack(u), 0.0)
        rest = B - k - S
        if rest:
            below = d[k + S :, :]
            groups = rest // S
            new = jnp.where(here[None], 0.0, below.reshape(groups, S, B))
            for i in range(S):
                v = w[i, i] * u[i]
                for m in range(i + 1, S):
                    v = v + w[m, i] * u[m]
                c = jnp.broadcast_to(below[:, k + i : k + i + 1], (rest, B)).reshape(groups, S, B)
                new = new - c * v[None]
            d[k + S :, :] = new.reshape(rest, B)


def factor_kernel(place, own, other, low_ref, inv_ref, a, d, up, wi):
    n = PANEL
    first = place[3] == 0
    block = lambda ref, i: ref[i * B : (i + 1) * B, :]
    p0 = [jnp.where(first, block(own, i), block(other, i)) for i in range(5)]
    p1 = [jnp.where(first, block(other, i), block(own, i)) for i in range(5)]
    lower = {
        (0, 0): p0[0], (1, 0): p0[1], (1, 1): p0[2],
        (2, 2): p1[0], (3, 2): p1[1], (3, 3): p1[2],
        (2, 0): p0[3], (3, 0): p0[4], (2, 1): p1[3].T, (3, 1): p1[4].T,
    }
    for (i, j), value in lower.items():
        a[i * B : (i + 1) * B, j * B : (j + 1) * B] = value
        if i != j:
            a[j * B : (j + 1) * B, i * B : (i + 1) * B] = value.T
    low_ref[...] = jnp.zeros_like(low_ref)
    inv_ref[...] = jnp.zeros_like(inv_ref)
    row = lax.broadcasted_iota(jnp.int32, (n, B), 0)

    def step(ob, _):
        at = pl.multiple_of(ob * B, B)
        blk = pl.ds(at, B)
        d[...] = a[blk, blk]
        factor_block(d, up, wi)
        w = wi[...]
        inv_ref[blk, blk] = w
        x = jnp.where(row >= at + B, dot(a[:, blk], w, ((1,), (1,))), 0.0)
        low_ref[:, blk] = x
        low_ref[blk, blk] = up[...].T
        a[...] = a[...] - dot(x, x, ((1,), (1,)))
        return 0

    lax.fori_loop(0, n // B, step, 0)
    size = B
    while size < n:
        for at in range(0, n, 2 * size):
            lo, hi = pl.ds(at, size), pl.ds(at + size, size)
            mid = dot(low_ref[hi, lo], inv_ref[lo, lo], ((1,), (0,)))
            inv_ref[hi, lo] = -dot(inv_ref[hi, hi], mid, ((1,), (0,)))
        size *= 2


def left_kernel(place, inv, own, other, x_ref, k_ref):
    first = place[3] == 0
    p0 = jnp.where(first, own[...], other[...])
    p1 = jnp.where(first, other[...], own[...])
    x_ref[...] = dot(p0, inv[:, :NB], ((1,), (1,))) + dot(p1, inv[:, NB:], ((1,), (1,)))
    k_ref[...] = dot(x_ref[...], inv[...], ((1,), (0,)))


def update_kernel(place, a, left, solved, low, here, behind, ahead, far0, far1, out):
    row, col, x = place[0], place[1], place[2]
    half = here.shape[1]
    out[...] = a[...]

    def apply(q, values, part, count):
        at = pl.multiple_of(jnp.where(q < 2, 0, half), half)
        depth = pl.multiple_of(jnp.where((q == 0) | (q == 3), 0, NB) + part, B)
        out[:, pl.ds(at, half)] -= dot(left[:, pl.ds(depth, count)], values[...], ((1,), (0,)))

    apply(x, here, 0, NB)
    apply(lax.rem(x + 3, 4), behind, 0, NB)
    apply(lax.rem(x + 1, 4), ahead, 0, NB)
    apply(lax.rem(x + 2, 4), far0, 0, NB // 2)
    apply(lax.rem(x + 2, 4), far1, NB // 2, NB // 2)

    @pl.when(col < 2)
    def _():
        out[:, :NB] = solved[:, pl.ds(pl.multiple_of(col * NB, NB), NB)]

    @pl.when(row < 2)
    def _():
        out[:NB, :] = jnp.zeros((NB, out.shape[1]), F32)

    @pl.when((row < 2) & (col < 2))
    def _():
        out[:NB, :NB] = low[pl.ds(pl.multiple_of(row * NB, NB), NB), pl.ds(pl.multiple_of(col * NB, NB), NB)]


def call(kernel, shapes, scratch, flops, *args):
    smem = pl.BlockSpec(memory_space=pltpu.SMEM)
    vmem = pl.BlockSpec(memory_space=pltpu.VMEM)
    moved = sum(int(np.prod(s)) for s in shapes) * 4 + sum(a.size for a in args) * 4
    outs = tuple(jax.ShapeDtypeStruct(s, F32) for s in shapes)
    return pl.pallas_call(
        kernel,
        out_shape=outs,
        in_specs=[smem] + [vmem] * (len(args) - 1),
        out_specs=tuple(vmem for _ in shapes),
        scratch_shapes=[pltpu.VMEM(s, F32) for s in scratch],
        compiler_params=pltpu.CompilerParams(vmem_limit_bytes=40 << 20),
        cost_estimate=pl.CostEstimate(flops=flops, bytes_accessed=moved, transcendentals=0),
    )(*args)


def on_device(matrix):
    row, col = lax.axis_index("row"), lax.axis_index("col")
    place = jnp.stack([row, col, row % NX, col % NK]).astype(jnp.int32)
    n, m = matrix.shape
    with jax.named_scope("corner"):
        corner = spread_corner(matrix[:NB, :NB], row, col)
    with jax.named_scope("rows"):
        rows = spread_rows(matrix[:NB, :])
    with jax.named_scope("cols"):
        cols = spread_cols(matrix[:, :NB])
    full = (PANEL, PANEL)
    low, inv = call(factor_kernel, [full, full], [full, (B, B), (B, B), (B, B)], 30_000_000_000, place, *corner)
    solved, left = call(left_kernel, [(n, PANEL), (n, PANEL)], [], 4 * n * PANEL * PANEL * 6, place, inv, *cols)
    (out,) = call(update_kernel, [(n, m)], [], 2 * n * m * PANEL * 6, place, matrix, left, solved, low, *rows)
    return out


def solution(mesh):
    return jax.shard_map(on_device, mesh=mesh, in_specs=(P("row", "col"),), out_specs=P("row", "col"), check_vma=False)
```

time: 1030 us -> 130 us (0.13)
  the two profiles are of different devices: /device:TPU:16 before, /device:TPU:24 now
where the time goes in v1:
time: 130 us; the launch traced here: 129 us
  starting transfers between devices  47.9 us (37%)
  Pallas kernels  40.3 us (31%)
  waiting for transfers between devices  33.9 us (26%)
  other arithmetic  6.34 us (5%)
    ppermute x26, starting transfers between devices, send(): return lax.ppermute(value, BOTH, pairs)  47.9 us
    pallas_call x3, Pallas kernels, call(): pl.pallas_call(kernel, out_shape=outs, in_specs=[smem] + [vmem] * (len(ar...  40.3 us
    ppermute x26, waiting for transfers between devices, send(): return lax.ppermute(value, BOTH, pairs)  33.9 us
  transfers between devices with their start and end apart: 26, of which 7 were waited for; matrix products, arithmetic and copies ran while one was open for 4% of the time, Pallas kernels for 26%

profile of v1, /device:TPU:24, one launch (start us, length us, event | category | flops | bytes accessed | tf_op | source)
XLA Modules:
  0.0 128.9 jit_solution(17931188215959338567)
XLA Ops:
  2.6 1.3 %collective-permute-start.1 = (f32[640,128]{1,0:T(8,128)S(1)}, f32[640,128]{1,0:T(8,128)S(1)}, u32[]{:S(2)}, u32[]{:S(2)}) collective-permute-start(f32[640,128]{1,0:T(8,128)S(1)} %maximum_select_fusion), channel_id=1, source_target_pairs={{0,6},{1,193},{16,22},{17,209}} | collective-permute-start | bytes 983048 | tf_op jit(solution)/shard_map/corner/ppermute | solution.py:37
  3.9 18.1 %collective-permute-done.1 = f32[640,128]{1,0:T(8,128)S(1)} collective-permute-done((f32[640,128]{1,0:T(8,128)S(1)}, f32[640,128]{1,0:T(8,128)S(1)}, u32[]{:S(2)}, u32[]{:S(2)}) %collective-permute-start.1) | collective-permute-done | bytes 327712 | tf_op jit(solution)/shard_map/corner/ppermute | solution.py:37
  22.0 1.3 %collective-permute-start.4 = (f32[640,128]{1,0:T(8,128)S(1)}, f32[640,128]{1,0:T(8,128)S(1)}, u32[]{:S(2)}, u32[]{:S(2)}) collective-permute-start(f32[640,128]{1,0:T(8,128)S(1)} %add_add_fusion.8), channel_id=1, source_target_pairs={{0,14},{1,449},{6,4},{16,30},{17,465},{22,20},{193,129},{209,145}} | collective-permute-start | bytes 983048 | tf_op jit(solution)/shard_map/corner/ppermute | solution.py:37
  23.4 1.3 %collective-permute-start.3 = (f32[640,128]{1,0:T(8,128)S(1)}, f32[640,128]{1,0:T(8,128)S(1)}, u32[]{:S(2)}, u32[]{:S(2)}) collective-permute-start(f32[640,128]{1,0:T(8,128)S(1)} %add_add_fusion.8), channel_id=1, source_target_pairs={{0,2},{1,65},{6,8},{10,12},{16,18},{17,81},{22,24},{26,28},{193,25... | collective-permute-start | bytes 983048 | tf_op jit(solution)/shard_map/corner/ppermute | solution.py:37
  24.7 2.1 %collective-permute-start.17 = (f32[256,512]{1,0:T(8,128)S(1)}, f32[256,512]{1,0:T(8,128)}, u32[]{:S(2)}, u32[]{:S(2)}) collective-permute-start(f32[256,512]{1,0:T(8,128)S(1)} %slice.40), channel_id=1, source_target_pairs={{0,48},{1,49},{2,50},{3,51},{4,52},{5,53},{6,54},{7,55},{8,56},{9,... | collective-permute-start | bytes 1572872 | tf_op jit(solution)/shard_map/rows/ppermute | solution.py:37
  27.9 1.3 %collective-permute-done.3 = f32[640,128]{1,0:T(8,128)S(1)} collective-permute-done((f32[640,128]{1,0:T(8,128)S(1)}, f32[640,128]{1,0:T(8,128)S(1)}, u32[]{:S(2)}, u32[]{:S(2)}) %collective-permute-start.3) | collective-permute-done | bytes 327712 | tf_op jit(solution)/shard_map/corner/ppermute | solution.py:37
  29.3 2.0 %collective-permute-start.6 = (f32[640,128]{1,0:T(8,128)S(1)}, f32[640,128]{1,0:T(8,128)}, u32[]{:S(2)}, u32[]{:S(2)}) collective-permute-start(f32[640,128]{1,0:T(8,128)S(1)} %add_add_fusion.7), channel_id=1, source_target_pairs={{0,320},{2,322},{4,324},{6,326},{8,328},{10,330},{12,332},{14,334}... | collective-permute-start | bytes 983048 | tf_op jit(solution)/shard_map/corner/ppermute | solution.py:37
  31.3 2.0 %collective-permute-start.5 = (f32[640,128]{1,0:T(8,128)S(1)}, f32[640,128]{1,0:T(8,128)}, u32[]{:S(2)}, u32[]{:S(2)}) collective-permute-start(f32[640,128]{1,0:T(8,128)S(1)} %add_add_fusion.7), channel_id=1, source_target_pairs={{0,192},{1,49},{2,194},{4,196},{6,198},{8,200},{10,202},{12,204},{... | collective-permute-start | bytes 983048 | tf_op jit(solution)/shard_map/corner/ppermute | solution.py:37
  33.4 2.1 %collective-permute-start.19 = (f32[256,512]{1,0:T(8,128)S(1)}, f32[256,512]{1,0:T(8,128)}, u32[]{:S(2)}, u32[]{:S(2)}) collective-permute-start(f32[256,512]{1,0:T(8,128)S(1)} %select_select_fusion), channel_id=1, source_target_pairs={{0,320},{1,321},{2,322},{3,323},{4,324},{5,325},{6,326},{7,327},{8... | collective-permute-start | bytes 1572872 | tf_op jit(solution)/shard_map/rows/ppermute | solution.py:37
  35.5 2.1 %collective-permute-start.18 = (f32[256,512]{1,0:T(8,128)S(1)}, f32[256,512]{1,0:T(8,128)}, u32[]{:S(2)}, u32[]{:S(2)}) collective-permute-start(f32[256,512]{1,0:T(8,128)S(1)} %select_select_fusion), channel_id=1, source_target_pairs={{0,192},{1,193},{2,194},{3,195},{4,196},{5,197},{6,198},{7,199},{8... | collective-permute-start | bytes 1572872 | tf_op jit(solution)/shard_map/rows/ppermute | solution.py:37
  38.1 2.6 %collective-permute-done.5 = f32[640,128]{1,0:T(8,128)} collective-permute-done((f32[640,128]{1,0:T(8,128)S(1)}, f32[640,128]{1,0:T(8,128)}, u32[]{:S(2)}, u32[]{:S(2)}) %collective-permute-start.5) | collective-permute-done | bytes 327712 | tf_op jit(solution)/shard_map/corner/ppermute | solution.py:37
  40.7 1.1 add_add_fusion.6
  41.8 2.0 %collective-permute-start.8 = (f32[640,128]{1,0:T(8,128)S(1)}, f32[640,128]{1,0:T(8,128)}, u32[]{:S(2)}, u32[]{:S(2)}) collective-permute-start(f32[640,128]{1,0:T(8,128)S(1)} %add_add_fusion.6), channel_id=1, source_target_pairs={{0,448},{1,11},{2,450},{4,452},{6,454},{8,456},{10,458},{12,460},{... | collective-permute-start | bytes 983048 | tf_op jit(solution)/shard_map/corner/ppermute | solution.py:37
  43.8 2.0 %collective-permute-start.7 = (f32[640,128]{1,0:T(8,128)S(1)}, f32[640,128]{1,0:T(8,128)}, u32[]{:S(2)}, u32[]{:S(2)}) collective-permute-start(f32[640,128]{1,0:T(8,128)S(1)} %add_add_fusion.6), channel_id=1, source_target_pairs={{0,64},{1,7},{2,66},{4,68},{6,70},{8,72},{10,74},{12,76},{14,78},{... | collective-permute-start | bytes 983048 | tf_op jit(solution)/shard_map/corner/ppermute | solution.py:37
  47.4 1.3 %collective-permute-start.12 = (f32[512,256]{1,0:T(8,128)}, f32[512,256]{1,0:T(8,128)S(1)}, u32[]{:S(2)}, u32[]{:S(2)}) collective-permute-start(f32[512,256]{1,0:T(8,128)} %slice_select_fusion), channel_id=1, source_target_pairs={{0,6},{1,7},{16,22},{17,23},{32,38},{33,39},{48,54},{49,55},{64,70... | collective-permute-start | bytes 1572872 | tf_op jit(solution)/shard_map/cols/ppermute | solution.py:37
  48.7 1.3 %add_add_fusion.1 = f32[256,512]{1,0:T(8,128)S(1)} fusion(f32[256,512]{1,0:T(8,128)} %collective-permute-done.19, f32[256,512]{1,0:T(8,128)S(1)} %select_select_fusion, f32[256,512]{1,0:T(8,128)} %collective-permute-done.18), kind=kLoop, calls=%fused_computation.1 | loop fusion | flops 262144 | bytes 2097152 | tf_op jit(solution)/shard_map/rows/add | solution.py:105
  50.1 1.3 %collective-permute-start.21 = (f32[256,512]{1,0:T(8,128)S(1)}, f32[256,512]{1,0:T(8,128)S(1)}, u32[]{:S(2)}, u32[]{:S(2)}) collective-permute-start(f32[256,512]{1,0:T(8,128)S(1)} %add_add_fusion.1), channel_id=1, source_target_pairs={{0,448},{1,449},{2,450},{3,451},{4,452},{5,453},{6,454},{7,455},{8... | collective-permute-start | bytes 1572872 | tf_op jit(solution)/shard_map/rows/ppermute | solution.py:37
  51.4 1.3 %collective-permute-start.20 = (f32[256,512]{1,0:T(8,128)S(1)}, f32[256,512]{1,0:T(8,128)S(1)}, u32[]{:S(2)}, u32[]{:S(2)}) collective-permute-start(f32[256,512]{1,0:T(8,128)S(1)} %add_add_fusion.1), channel_id=1, source_target_pairs={{0,64},{1,65},{2,66},{3,67},{4,68},{5,69},{6,70},{7,71},{8,72},{9,... | collective-permute-start | bytes 1572872 | tf_op jit(solution)/shard_map/rows/ppermute | solution.py:37
  52.7 1.1 add_add_fusion.5
  54.6 1.9 %collective-permute-start.9 = (f32[640,128]{1,0:T(8,128)S(1)}, f32[640,128]{1,0:T(8,128)S(1)}, u32[]{:S(2)}, u32[]{:S(2)}) collective-permute-start(f32[640,128]{1,0:T(8,128)S(1)} %add_add_fusion.5), channel_id=1, source_target_pairs={{0,48},{1,3},{2,50},{4,52},{6,54},{7,9},{8,56},{10,58},{11,13},{12... | collective-permute-start | bytes 983048 | tf_op jit(solution)/shard_map/corner/ppermute | solution.py:37
  56.5 9.7 %collective-permute-done.12 = f32[512,256]{1,0:T(8,128)S(1)} collective-permute-done((f32[512,256]{1,0:T(8,128)}, f32[512,256]{1,0:T(8,128)S(1)}, u32[]{:S(2)}, u32[]{:S(2)}) %collective-permute-start.12) | collective-permute-done | bytes 524320 | tf_op jit(solution)/shard_map/cols/ppermute | solution.py:37
  66.3 1.3 %collective-permute-start.15 = (f32[512,256]{1,0:T(8,128)S(1)}, f32[512,256]{1,0:T(8,128)S(1)}, u32[]{:S(2)}, u32[]{:S(2)}) collective-permute-start(f32[512,256]{1,0:T(8,128)S(1)} %add_add_fusion.3), channel_id=1, source_target_pairs={{0,14},{1,15},{6,4},{7,5},{16,30},{17,31},{22,20},{23,21},{32,46},... | collective-permute-start | bytes 1572872 | tf_op jit(solution)/shard_map/cols/ppermute | solution.py:37
  67.6 1.3 %collective-permute-start.14 = (f32[512,256]{1,0:T(8,128)S(1)}, f32[512,256]{1,0:T(8,128)S(1)}, u32[]{:S(2)}, u32[]{:S(2)}) collective-permute-start(f32[512,256]{1,0:T(8,128)S(1)} %add_add_fusion.3), channel_id=1, source_target_pairs={{0,2},{1,3},{6,8},{7,9},{10,12},{11,13},{16,18},{17,19},{22,24},{2... | collective-permute-start | bytes 1572872 | tf_op jit(solution)/shard_map/cols/ppermute | solution.py:37
  69.1 1.9 %collective-permute-start.22 = (f32[256,512]{1,0:T(8,128)S(1)}, f32[256,512]{1,0:T(8,128)S(1)}, u32[]{:S(2)}, u32[]{:S(2)}) collective-permute-start(f32[256,512]{1,0:T(8,128)S(1)} %add_add_fusion.here), channel_id=1, source_target_pairs={{0,16},{1,17},{2,18},{3,19},{4,20},{5,21},{6,22},{7,23},{8,24},{9,... | collective-permute-start | bytes 1572872 | tf_op jit(solution)/shard_map/rows/ppermute | solution.py:37
  71.1 5.1 %collective-permute-start.23 = (f32[256,512]{1,0:T(8,128)S(1)}, f32[256,512]{1,0:T(8,128)S(1)}, u32[]{:S(2)}, u32[]{:S(2)}) collective-permute-start(f32[256,512]{1,0:T(8,128)S(1)} %add_add_fusion.here), channel_id=1, source_target_pairs={{0,48},{1,49},{2,50},{3,51},{4,52},{5,53},{6,54},{7,55},{8,56},{9,... | collective-permute-start | bytes 1572872 | tf_op jit(solution)/shard_map/rows/ppermute | solution.py:37
  76.3 1.9 %collective-permute-start.11 = (f32[640,128]{1,0:T(8,128)S(1)}, f32[640,128]{1,0:T(8,128)S(1)}, u32[]{:S(2)}, u32[]{:S(2)}) collective-permute-start(f32[640,128]{1,0:T(8,128)S(1)} %add_add_fusion.4.own), channel_id=1, source_target_pairs={{0,1},{1,0},{2,3},{3,2},{4,5},{5,4},{6,7},{7,6},{8,9},{9,8},{10,11... | collective-permute-start | bytes 983048 | tf_op jit(solution)/shard_map/corner/ppermute | solution.py:37
  78.4 2.4 %collective-permute-start.16 = (f32[512,256]{1,0:T(8,128)S(1)}, f32[512,256]{1,0:T(8,128)S(1)}, u32[]{:S(2)}, u32[]{:S(2)}) collective-permute-start(f32[512,256]{1,0:T(8,128)S(1)} %add_add_fusion.2.own), channel_id=1, source_target_pairs={{0,1},{1,0},{2,3},{3,2},{4,5},{5,4},{6,7},{7,6},{8,9},{9,8},{10,11... | collective-permute-start | bytes 1572872 | tf_op jit(solution)/shard_map/cols/ppermute | solution.py:37
  81.4 1.9 %collective-permute-start.24 = (f32[128,512]{1,0:T(8,128)S(1)}, f32[128,512]{1,0:T(8,128)S(1)}, u32[]{:S(2)}, u32[]{:S(2)}) collective-permute-start(f32[128,512]{1,0:T(8,128)S(1)} %slice.45), channel_id=1, source_target_pairs={{0,16},{1,17},{2,18},{3,19},{4,20},{5,21},{6,22},{7,23},{8,24},{9,... | collective-permute-start | bytes 786440 | tf_op jit(solution)/shard_map/rows/ppermute | solution.py:37
  83.4 5.1 %collective-permute-start.25 = (f32[128,512]{1,0:T(8,128)S(1)}, f32[128,512]{1,0:T(8,128)S(1)}, u32[]{:S(2)}, u32[]{:S(2)}) collective-permute-start(f32[128,512]{1,0:T(8,128)S(1)} %slice.46), channel_id=1, source_target_pairs={{0,48},{1,49},{2,50},{3,51},{4,52},{5,53},{6,54},{7,55},{8,56},{9,... | collective-permute-start | bytes 786440 | tf_op jit(solution)/shard_map/rows/ppermute | solution.py:37
  88.5 29.5 %shard_map.17 = (f32[512,512]{1,0:T(8,128)S(1)}, f32[512,512]{1,0:T(8,128)S(1)}) custom-call(s32[4]{0:T(128)S(1)} %pad_add_fusion.place, f32[640,128]{1,0:T(8,128)S(1)} %add_add_fusion.4.own, f32[640,128]{1,0:T(8,128)S(1)} %collective-permute-done.11.other), custom_call_target="tpu_custom_call" | custom-call | flops 30000001024 | bytes 2752528 | tf_op jit(solution)/shard_map/pallas_call | solution.py:260
  118.1 4.1 %shard_map.18 = (f32[512,512]{1,0:T(8,128)S(1)}, f32[512,512]{1,0:T(8,128)S(1)}) custom-call(s32[4]{0:T(128)S(1)} %pad_add_fusion.place, f32[512,512]{1,0:T(8,128)S(1)} %get-tuple-element.9.inv, f32[512,256]{1,0:T(8,128)S(1)} %add_add_fusion.2.own, f32[512,256]{1,0:T(8,128)S(1)} %collective-permute-done.16.other), custom_call_target="tpu_custom_call" | custom-call | flops 3221225472 | bytes 4194320 | tf_op jit(solution)/shard_map/pallas_call | solution.py:260
  122.2 6.7 %shard_map.19 = f32[512,1024]{1,0:T(8,128)} custom-call(s32[4]{0:T(128)S(1)} %pad_add_fusion.place, f32[512,1024]{1,0:T(8,128)S(1)} %copy-done, f32[512,512]{1,0:T(8,128)S(1)} %get-tuple-element.10.left, f32[512,512]{1,0:T(8,128)S(1)} %get-tuple-element.11.solved, f32[512,512]{1,0:T(8,128)S(1)} %get-tuple-element.12.low, f32[256,512]{1,0:T(8,128)S(1)} %add_add_fusion.here, ...), custom_call_target="tpu_custom_call" | custom-call | flops 3221225472 | bytes 9437200 | tf_op jit(solution)/shard_map/pallas_call | solution.py:260
  (45 shorter events, 7.7 us)
Async XLA Ops:
  0.0 24.7 %copy-start = (f32[512,1024]{1,0:T(8,128)S(1)}, f32[512,1024]{1,0:T(8,128)}, u32[]{:S(2)}) copy-start(f32[512,1024]{1,0:T(8,128)} %a.1) | copy-start | bytes 6291460
  1.1 0.7 collective-permute-start
  1.9 2.0 %collective-permute-start.2 = (f32[640,128]{1,0:T(8,128)S(1)}, f32[640,128]{1,0:T(8,128)S(1)}, u32[]{:S(2)}, u32[]{:S(2)}) collective-permute-start(f32[640,128]{1,0:T(8,128)S(1)} %maximum_select_fusion), channel_id=1, source_target_pairs={{0,10},{1,321},{16,26},{17,337}} | collective-permute-start | bytes 983048 | tf_op jit(solution)/shard_map/corner/ppermute | solution.py:37
  2.6 19.4 %collective-permute-start.1 = (f32[640,128]{1,0:T(8,128)S(1)}, f32[640,128]{1,0:T(8,128)S(1)}, u32[]{:S(2)}, u32[]{:S(2)}) collective-permute-start(f32[640,128]{1,0:T(8,128)S(1)} %maximum_select_fusion), channel_id=1, source_target_pairs={{0,6},{1,193},{16,22},{17,209}} | collective-permute-start | bytes 983048 | tf_op jit(solution)/shard_map/corner/ppermute | solution.py:37
  22.0 5.9 %collective-permute-start.4 = (f32[640,128]{1,0:T(8,128)S(1)}, f32[640,128]{1,0:T(8,128)S(1)}, u32[]{:S(2)}, u32[]{:S(2)}) collective-permute-start(f32[640,128]{1,0:T(8,128)S(1)} %add_add_fusion.8), channel_id=1, source_target_pairs={{0,14},{1,449},{6,4},{16,30},{17,465},{22,20},{193,129},{209,145}} | collective-permute-start | bytes 983048 | tf_op jit(solution)/shard_map/corner/ppermute | solution.py:37
  23.4 5.9 %collective-permute-start.3 = (f32[640,128]{1,0:T(8,128)S(1)}, f32[640,128]{1,0:T(8,128)S(1)}, u32[]{:S(2)}, u32[]{:S(2)}) collective-permute-start(f32[640,128]{1,0:T(8,128)S(1)} %add_add_fusion.8), channel_id=1, source_target_pairs={{0,2},{1,65},{6,8},{10,12},{16,18},{17,81},{22,24},{26,28},{193,25... | collective-permute-start | bytes 983048 | tf_op jit(solution)/shard_map/corner/ppermute | solution.py:37
  24.7 8.6 %collective-permute-start.17 = (f32[256,512]{1,0:T(8,128)S(1)}, f32[256,512]{1,0:T(8,128)}, u32[]{:S(2)}, u32[]{:S(2)}) collective-permute-start(f32[256,512]{1,0:T(8,128)S(1)} %slice.40), channel_id=1, source_target_pairs={{0,48},{1,49},{2,50},{3,51},{4,52},{5,53},{6,54},{7,55},{8,56},{9,... | collective-permute-start | bytes 1572872 | tf_op jit(solution)/shard_map/rows/ppermute | solution.py:37
  29.3 8.8 %collective-permute-start.6 = (f32[640,128]{1,0:T(8,128)S(1)}, f32[640,128]{1,0:T(8,128)}, u32[]{:S(2)}, u32[]{:S(2)}) collective-permute-start(f32[640,128]{1,0:T(8,128)S(1)} %add_add_fusion.7), channel_id=1, source_target_pairs={{0,320},{2,322},{4,324},{6,326},{8,328},{10,330},{12,332},{14,334}... | collective-permute-start | bytes 983048 | tf_op jit(solution)/shard_map/corner/ppermute | solution.py:37
  31.3 9.4 %collective-permute-start.5 = (f32[640,128]{1,0:T(8,128)S(1)}, f32[640,128]{1,0:T(8,128)}, u32[]{:S(2)}, u32[]{:S(2)}) collective-permute-start(f32[640,128]{1,0:T(8,128)S(1)} %add_add_fusion.7), channel_id=1, source_target_pairs={{0,192},{1,49},{2,194},{4,196},{6,198},{8,200},{10,202},{12,204},{... | collective-permute-start | bytes 983048 | tf_op jit(solution)/shard_map/corner/ppermute | solution.py:37
  33.4 14.0 %collective-permute-start.19 = (f32[256,512]{1,0:T(8,128)S(1)}, f32[256,512]{1,0:T(8,128)}, u32[]{:S(2)}, u32[]{:S(2)}) collective-permute-start(f32[256,512]{1,0:T(8,128)S(1)} %select_select_fusion), channel_id=1, source_target_pairs={{0,320},{1,321},{2,322},{3,323},{4,324},{5,325},{6,326},{7,327},{8... | collective-permute-start | bytes 1572872 | tf_op jit(solution)/shard_map/rows/ppermute | solution.py:37
  35.5 13.2 %collective-permute-start.18 = (f32[256,512]{1,0:T(8,128)S(1)}, f32[256,512]{1,0:T(8,128)}, u32[]{:S(2)}, u32[]{:S(2)}) collective-permute-start(f32[256,512]{1,0:T(8,128)S(1)} %select_select_fusion), channel_id=1, source_target_pairs={{0,192},{1,193},{2,194},{3,195},{4,196},{5,197},{6,198},{7,199},{8... | collective-permute-start | bytes 1572872 | tf_op jit(solution)/shard_map/rows/ppermute | solution.py:37
  41.8 9.6 %collective-permute-start.8 = (f32[640,128]{1,0:T(8,128)S(1)}, f32[640,128]{1,0:T(8,128)}, u32[]{:S(2)}, u32[]{:S(2)}) collective-permute-start(f32[640,128]{1,0:T(8,128)S(1)} %add_add_fusion.6), channel_id=1, source_target_pairs={{0,448},{1,11},{2,450},{4,452},{6,454},{8,456},{10,458},{12,460},{... | collective-permute-start | bytes 983048 | tf_op jit(solution)/shard_map/corner/ppermute | solution.py:37
  43.8 8.9 %collective-permute-start.7 = (f32[640,128]{1,0:T(8,128)S(1)}, f32[640,128]{1,0:T(8,128)}, u32[]{:S(2)}, u32[]{:S(2)}) collective-permute-start(f32[640,128]{1,0:T(8,128)S(1)} %add_add_fusion.6), channel_id=1, source_target_pairs={{0,64},{1,7},{2,66},{4,68},{6,70},{8,72},{10,74},{12,76},{14,78},{... | collective-permute-start | bytes 983048 | tf_op jit(solution)/shard_map/corner/ppermute | solution.py:37
  46.7 7.9 %collective-permute-start.13 = (f32[512,256]{1,0:T(8,128)}, f32[512,256]{1,0:T(8,128)S(1)}, u32[]{:S(2)}, u32[]{:S(2)}) collective-permute-start(f32[512,256]{1,0:T(8,128)} %slice_select_fusion), channel_id=1, source_target_pairs={{0,10},{1,11},{16,26},{17,27},{32,42},{33,43},{48,58},{49,59},{64,... | collective-permute-start | bytes 1572872 | tf_op jit(solution)/shard_map/cols/ppermute | solution.py:37
  47.4 18.7 %collective-permute-start.12 = (f32[512,256]{1,0:T(8,128)}, f32[512,256]{1,0:T(8,128)S(1)}, u32[]{:S(2)}, u32[]{:S(2)}) collective-permute-start(f32[512,256]{1,0:T(8,128)} %slice_select_fusion), channel_id=1, source_target_pairs={{0,6},{1,7},{16,22},{17,23},{32,38},{33,39},{48,54},{49,55},{64,70... | collective-permute-start | bytes 1572872 | tf_op jit(solution)/shard_map/cols/ppermute | solution.py:37
  50.1 17.5 %collective-permute-start.21 = (f32[256,512]{1,0:T(8,128)S(1)}, f32[256,512]{1,0:T(8,128)S(1)}, u32[]{:S(2)}, u32[]{:S(2)}) collective-permute-start(f32[256,512]{1,0:T(8,128)S(1)} %add_add_fusion.1), channel_id=1, source_target_pairs={{0,448},{1,449},{2,450},{3,451},{4,452},{5,453},{6,454},{7,455},{8... | collective-permute-start | bytes 1572872 | tf_op jit(solution)/shard_map/rows/ppermute | solution.py:37
  51.4 17.5 %collective-permute-start.20 = (f32[256,512]{1,0:T(8,128)S(1)}, f32[256,512]{1,0:T(8,128)S(1)}, u32[]{:S(2)}, u32[]{:S(2)}) collective-permute-start(f32[256,512]{1,0:T(8,128)S(1)} %add_add_fusion.1), channel_id=1, source_target_pairs={{0,64},{1,65},{2,66},{3,67},{4,68},{5,69},{6,70},{7,71},{8,72},{9,... | collective-permute-start | bytes 1572872 | tf_op jit(solution)/shard_map/rows/ppermute | solution.py:37
  53.9 17.2 %collective-permute-start.10 = (f32[640,128]{1,0:T(8,128)S(1)}, f32[640,128]{1,0:T(8,128)S(1)}, u32[]{:S(2)}, u32[]{:S(2)}) collective-permute-start(f32[640,128]{1,0:T(8,128)S(1)} %add_add_fusion.5), channel_id=1, source_target_pairs={{1,15},{7,5},{17,31},{23,21},{33,47},{39,37},{49,63},{55,53},{65,7... | collective-permute-start | bytes 983048 | tf_op jit(solution)/shard_map/corner/ppermute | solution.py:37
  54.6 21.6 %collective-permute-start.9 = (f32[640,128]{1,0:T(8,128)S(1)}, f32[640,128]{1,0:T(8,128)S(1)}, u32[]{:S(2)}, u32[]{:S(2)}) collective-permute-start(f32[640,128]{1,0:T(8,128)S(1)} %add_add_fusion.5), channel_id=1, source_target_pairs={{0,48},{1,3},{2,50},{4,52},{6,54},{7,9},{8,56},{10,58},{11,13},{12... | collective-permute-start | bytes 983048 | tf_op jit(solution)/shard_map/corner/ppermute | solution.py:37
  66.3 12.0 %collective-permute-start.15 = (f32[512,256]{1,0:T(8,128)S(1)}, f32[512,256]{1,0:T(8,128)S(1)}, u32[]{:S(2)}, u32[]{:S(2)}) collective-permute-start(f32[512,256]{1,0:T(8,128)S(1)} %add_add_fusion.3), channel_id=1, source_target_pairs={{0,14},{1,15},{6,4},{7,5},{16,30},{17,31},{22,20},{23,21},{32,46},... | collective-permute-start | bytes 1572872 | tf_op jit(solution)/shard_map/cols/ppermute | solution.py:37
  67.6 10.7 %collective-permute-start.14 = (f32[512,256]{1,0:T(8,128)S(1)}, f32[512,256]{1,0:T(8,128)S(1)}, u32[]{:S(2)}, u32[]{:S(2)}) collective-permute-start(f32[512,256]{1,0:T(8,128)S(1)} %add_add_fusion.3), channel_id=1, source_target_pairs={{0,2},{1,3},{6,8},{7,9},{10,12},{11,13},{16,18},{17,19},{22,24},{2... | collective-permute-start | bytes 1572872 | tf_op jit(solution)/shard_map/cols/ppermute | solution.py:37
  69.1 12.3 %collective-permute-start.22 = (f32[256,512]{1,0:T(8,128)S(1)}, f32[256,512]{1,0:T(8,128)S(1)}, u32[]{:S(2)}, u32[]{:S(2)}) collective-permute-start(f32[256,512]{1,0:T(8,128)S(1)} %add_add_fusion.here), channel_id=1, source_target_pairs={{0,16},{1,17},{2,18},{3,19},{4,20},{5,21},{6,22},{7,23},{8,24},{9,... | collective-permute-start | bytes 1572872 | tf_op jit(solution)/shard_map/rows/ppermute | solution.py:37
  71.1 12.3 %collective-permute-start.23 = (f32[256,512]{1,0:T(8,128)S(1)}, f32[256,512]{1,0:T(8,128)S(1)}, u32[]{:S(2)}, u32[]{:S(2)}) collective-permute-start(f32[256,512]{1,0:T(8,128)S(1)} %add_add_fusion.here), channel_id=1, source_target_pairs={{0,48},{1,49},{2,50},{3,51},{4,52},{5,53},{6,54},{7,55},{8,56},{9,... | collective-permute-start | bytes 1572872 | tf_op jit(solution)/shard_map/rows/ppermute | solution.py:37
  76.3 12.3 %collective-permute-start.11 = (f32[640,128]{1,0:T(8,128)S(1)}, f32[640,128]{1,0:T(8,128)S(1)}, u32[]{:S(2)}, u32[]{:S(2)}) collective-permute-start(f32[640,128]{1,0:T(8,128)S(1)} %add_add_fusion.4.own), channel_id=1, source_target_pairs={{0,1},{1,0},{2,3},{3,2},{4,5},{5,4},{6,7},{7,6},{8,9},{9,8},{10,11... | collective-permute-start | bytes 983048 | tf_op jit(solution)/shard_map/corner/ppermute | solution.py:37
  78.4 39.7 %collective-permute-start.16 = (f32[512,256]{1,0:T(8,128)S(1)}, f32[512,256]{1,0:T(8,128)S(1)}, u32[]{:S(2)}, u32[]{:S(2)}) collective-permute-start(f32[512,256]{1,0:T(8,128)S(1)} %add_add_fusion.2.own), channel_id=1, source_target_pairs={{0,1},{1,0},{2,3},{3,2},{4,5},{5,4},{6,7},{7,6},{8,9},{9,8},{10,11... | collective-permute-start | bytes 1572872 | tf_op jit(solution)/shard_map/cols/ppermute | solution.py:37
  81.4 40.8 %collective-permute-start.24 = (f32[128,512]{1,0:T(8,128)S(1)}, f32[128,512]{1,0:T(8,128)S(1)}, u32[]{:S(2)}, u32[]{:S(2)}) collective-permute-start(f32[128,512]{1,0:T(8,128)S(1)} %slice.45), channel_id=1, source_target_pairs={{0,16},{1,17},{2,18},{3,19},{4,20},{5,21},{6,22},{7,23},{8,24},{9,... | collective-permute-start | bytes 786440 | tf_op jit(solution)/shard_map/rows/ppermute | solution.py:37
  83.4 38.8 %collective-permute-start.25 = (f32[128,512]{1,0:T(8,128)S(1)}, f32[128,512]{1,0:T(8,128)S(1)}, u32[]{:S(2)}, u32[]{:S(2)}) collective-permute-start(f32[128,512]{1,0:T(8,128)S(1)} %slice.46), channel_id=1, source_target_pairs={{0,48},{1,49},{2,50},{3,51},{4,52},{5,53},{6,54},{7,55},{8,56},{9,... | collective-permute-start | bytes 786440 | tf_op jit(solution)/shard_map/rows/ppermute | solution.py:37

commit v2 on v1

v2 whole, which is shorter than its diff:
```python
import functools

import jax
import jax.numpy as jnp
import numpy as np
from jax import lax
from jax.experimental import pallas as pl
from jax.experimental.pallas import tpu as pltpu
from jax.sharding import PartitionSpec as P

NB = 256
PANEL = 512
NZ, NX, NY, NK = 8, 4, 8, 2
B = 128
S = 8
F32 = jnp.float32
BOTH = ("row", "col")


def dot(a, b, dims):
    return lax.dot_general(a, b, (dims, ((), ())), precision=lax.Precision.HIGHEST, preferred_element_type=F32)


def device(z, x, y, k):
    return (((z % NZ) * NX + x % NX) * NY + y % NY) * NK + k


DEVICES = [(z, x, y, k) for z in range(NZ) for x in range(NX) for y in range(NY) for k in range(NK)]


def send(value, target):
    pairs = []
    for at in DEVICES:
        to = target(*at)
        if to is not None:
            pairs.append((device(*at), device(*to)))
    return lax.ppermute(value, BOTH, pairs)


HOPS = [({0: 3}, {0: 5}), ({0: 1, 3: 4, 5: 6}, {0: 7, 3: 2})]


def along_y(part, where=lambda z, x, k: True):
    return lambda z, x, y, k: (z, x, part[y], k) if y in part and where(z, x, k) else None


def along_z(part, where=lambda x, y, k: True):
    return lambda z, x, y, k: (part[z], x, y, k) if z in part and where(x, y, k) else None


def along_x(part, where=lambda z, y, k: True):
    return lambda z, x, y, k: (z, part[x], y, k) if x in part and where(z, y, k) else None


def other_core(z, x, y, k):
    return z, x, y, 1 - k


def spread(value, targets, earlier=None):
    got = [send(value, target) for target in targets]
    if earlier is not None:
        got[0] = after(got[0], earlier)
    return functools.reduce(jnp.add, got, value)


def after(value, *earlier):
    return lax.optimization_barrier((value, *earlier))[0]


def corner_piece(block, row, col):
    blocks = [block[:B, :B], block[B:, :B], block[B:, B:]]
    first, second = [jnp.where(col == 0, x, y) for x, y in zip(blocks, blocks[1:])]
    mine = [jnp.where(row == col, t, h) for t, h in zip(blocks, (first, second, second))]
    return jnp.where((row < 2) & (col < 2), jnp.concatenate(mine), 0.0)


def pin(values, *earlier):
    return lax.optimization_barrier((tuple(values), earlier))[0]


def corner_tree(piece, quarter, sent, x_index, core):
    rounds = [
        [along_z(h, lambda x, y, k: x < 2 and y == 0) for h in HOPS[0]],
        [along_z(h, lambda x, y, k: x < 2 and y == 0) for h in HOPS[1]],
        [along_y(h, lambda z, x, k: x < 2) for h in HOPS[0]],
        [along_y(h, lambda z, x, k: x < 2) for h in HOPS[1]],
    ]
    piece = spread(piece, rounds[0])
    piece = spread(piece, rounds[1], sent)
    quarter = quarter(sent)
    piece = spread(piece, rounds[2])
    quarter = spread(quarter, [along_z(h) for h in HOPS[0]])
    piece = spread(piece, rounds[3], quarter)
    quarter = spread(quarter, [along_z(h) for h in HOPS[1]])
    swap, near, far = [send(piece, along_x(part)) for part in ({0: 1, 1: 0}, {0: 3, 1: 2}, {0: 2, 1: 3})]
    pick = lambda *choices: functools.reduce(lambda v, i: jnp.where(x_index == i, choices[i], v), (1, 2, 3), choices[0])
    even, odd = pick(piece, swap, far, near), pick(swap, piece, near, far)
    triangle = jnp.where(core == 0, even, odd)
    rest = jnp.where(core == 0, odd, even)[: 2 * B]
    mine = jnp.concatenate([triangle, rest])
    return piece, (mine, send(mine, other_core)), quarter


def factor_block(d, up, inv, tasks=()):
    lane = lax.broadcasted_iota(jnp.int32, (S, B), 1)
    sub = lax.broadcasted_iota(jnp.int32, (S, B), 0)
    panels = B // S
    tasks = list(tasks)

    def stack(rows):
        out = rows[0]
        for i in range(1, S):
            out = jnp.where(sub == i, rows[i], out)
        return out

    for done, k in enumerate(range(0, B, S)):
        here = (lane >= k) & (lane < k + S)
        p = [jnp.broadcast_to(d[k + i : k + i + 1, :], (S, B)) for i in range(S)]
        spare = B + done % 2 * S * S
        for j in range(S):
            d[spare + j * S : spare + (j + 1) * S, :] = jnp.broadcast_to(d[k : k + S, k + j : k + j + 1], (S, B))
        element = lambda i, j: d[spare + j * S + i : spare + j * S + i + 1, :]
        s = {(i, j): jnp.broadcast_to(element(i, j), (S, B)) for i in range(S) for j in range(i + 1)}
        r, w = [], {}
        for j in range(S):
            r.append(lax.rsqrt(s[j, j]))
            for i in range(j + 1, S):
                s[i, j] = s[i, j] * r[j]
            for i in range(j + 1, S):
                for m in range(j + 1, i + 1):
                    s[i, m] = s[i, m] - s[i, j] * s[m, j]
            w[j, j] = r[j]
            for m in range(j):
                acc = s[j, m] * w[m, m]
                for q in range(m + 1, j):
                    acc = acc + s[j, q] * w[q, m]
                w[j, m] = -r[j] * acc
        q = [jnp.where(here, jnp.where(lane == k + i, 1.0, 0.0), p[i]) for i in range(S)]
        u, t = [], []
        for i in range(S):
            a = w[i, 0] * q[0]
            b = w[i, 0] * p[0]
            for m in range(1, i + 1):
                a = a + w[i, m] * q[m]
                b = b + w[i, m] * p[m]
            u.append(a)
            t.append(b)
        up[k : k + S, :] = jnp.where(lane >= k + sub, stack(t), 0.0)
        inv[k : k + S, :] = jnp.where(lane <= k + sub, stack(u), 0.0)
        rest = B - k - S
        if rest:
            below = d[k + S : B, :]
            groups = rest // S
            new = jnp.where(here[None], 0.0, below.reshape(groups, S, B))
            for i in range(S):
                v = w[i, i] * u[i]
                for m in range(i + 1, S):
                    v = v + w[m, i] * u[m]
                c = jnp.broadcast_to(below[:, k + i : k + i + 1], (rest, B)).reshape(groups, S, B)
                new = new - c * v[None]
            d[k + S : B, :] = new.reshape(rest, B)
        for task in tasks[len(tasks) * done // panels : len(tasks) * (done + 1) // panels]:
            task()


def at(i, j):
    return pl.ds(i * B, B), pl.ds(j * B, B)


def outer(a, b):
    return dot(a, b, ((1,), (1,)))


def inner(a, b):
    return dot(a, b, ((1,), (0,)))


def below_task(a, low, inv, i, j):
    def task():
        low[at(i, j)] = outer(a[at(i, j)], inv[at(j, j)])

    return task


def trail_task(a, low, i, j, p):
    def task():
        a[at(i, j)] = a[at(i, j)] - outer(low[at(i, p)], low[at(j, p)])

    return task


def upto(i):
    return pl.ds(0, i * B)


def gather_task(low, inv, mid, i):
    def task():
        mid[:, upto(i)] = inner(low[pl.ds(i * B, B), upto(i)], inv[upto(i), upto(i)])

    return task


def invert_task(inv, mid, i):
    def task():
        inv[pl.ds(i * B, B), upto(i)] = -inner(inv[at(i, i)], mid[:, upto(i)])

    return task


def factor_step(i, low, inv, a, d, up, tasks):
    d[:B, :] = a[at(i, i)]
    factor_block(d, up, inv.at[at(i, i)], tasks)
    low[at(i, i)] = up[...].T
    if i < 3:
        below_task(a, low, inv, i + 1, i)()
        trail_task(a, low, i + 1, i + 1, i)()


def first_kernel(place, own, other, low, inv, a, d, up):
    first = place[3] == 0
    block = lambda ref, i: ref[i * B : (i + 1) * B, :]
    p0 = [jnp.where(first, block(own, i), block(other, i)) for i in range(5)]
    p1 = [jnp.where(first, block(other, i), block(own, i)) for i in range(5)]
    lower = {
        (0, 0): p0[0], (1, 0): p0[1], (1, 1): p0[2],
        (2, 2): p1[0], (3, 2): p1[1], (3, 3): p1[2],
        (2, 0): p0[3], (3, 0): p0[4], (2, 1): p1[3].T, (3, 1): p1[4].T,
    }
    for (i, j), value in lower.items():
        a[at(i, j)] = value
    low[...] = jnp.zeros_like(low)
    inv[...] = jnp.zeros_like(inv)
    factor_step(0, low, inv, a, d, up, ())


def next_kernel(i, low_in, inv_in, a_in, low, inv, a, d, up, mid):
    low[...] = low_in[...]
    inv[...] = inv_in[...]
    a[...] = a_in[...]
    if i == 1:
        tasks = [below_task(a, low, inv, m, 0) for m in (2, 3)]
        tasks += [trail_task(a, low, m, n, 0) for m, n in ((2, 1), (2, 2), (3, 1), (3, 2), (3, 3))]
        tasks += [gather_task(low, inv, mid, 1)]
    else:
        tasks = [below_task(a, low, inv, 3, 1), trail_task(a, low, 3, 2, 1), trail_task(a, low, 3, 3, 1), gather_task(low, inv, mid, 2)]
    factor_step(i, low, inv, a, d, up, tasks)
    invert_task(inv, mid, i)()


def finish_kernel(place, own, other, low_in, inv_in, a_in, low, solved, left, inv, p, d, up, mid):
    first = place[3] == 0
    low[...] = low_in[...]
    inv[...] = inv_in[...]
    p[:, :NB] = jnp.where(first, own[...], other[...])
    p[:, NB:] = jnp.where(first, other[...], own[...])
    left[...] = jnp.zeros_like(left)
    cols = lambda j: (slice(None), pl.ds(j * B, B))

    def solve(j):
        def task():
            solved[cols(j)] = outer(p[cols(j)], inv[at(j, j)])

        return task

    def panel(i, j):
        def task():
            p[cols(i)] = p[cols(i)] - outer(solved[cols(j)], low[at(i, j)])

        return task

    def add(j):
        def task():
            left[:, upto(j + 1)] = left[:, upto(j + 1)] + inner(solved[cols(j)], inv[pl.ds(j * B, B), upto(j + 1)])

        return task

    tasks = [
        solve(0), panel(1, 0), panel(2, 0), panel(3, 0), solve(1), gather_task(low, inv, mid, 3), panel(2, 1), panel(3, 1),
        add(0), solve(2), add(1), panel(3, 2), add(2),
    ]
    d[:B, :] = a_in[at(3, 3)]
    factor_block(d, up, inv.at[at(3, 3)], tasks)
    low[at(3, 3)] = up[...].T
    solve(3)()
    invert_task(inv, mid, 3)()
    add(3)()


def split(value):
    high = value.astype(jnp.bfloat16)
    return high, (value - high.astype(F32)).astype(jnp.bfloat16)


def update_kernel(place, a, left, solved, low, here, beside, across, opposite, out, high, rest):
    row, col, x = place[0], place[1], place[2]
    half = here.shape[1]

    @pl.when(pl.program_id(0) == 0)
    def _():
        for flip, values in ((0, here), (1, beside), (3, across), (2, opposite)):
            q = x ^ flip
            down = jnp.where((q == 1) | (q == 2), NB, 0)
            over = jnp.where(q >= 2, half, 0)
            spot = pl.ds(pl.multiple_of(down, NB), NB), pl.ds(pl.multiple_of(over, half), half)
            high[spot], rest[spot] = split(values[...])

    lh, ll = split(left[...])
    one = lambda u, v: lax.dot_general(u, v, (((1,), (0,)), ((), ())), preferred_element_type=F32)
    product = one(lh, high[...]) + (one(lh, rest[...]) + one(ll, high[...]))
    out[...] = a[...] - product

    @pl.when(col < 2)
    def _():
        out[:, :NB] = solved[:, pl.ds(pl.multiple_of(col * NB, NB), NB)]

    mine = out.shape[0]
    start = pl.program_id(0) * mine

    @pl.when((row < 2) & (start < NB))
    def _():
        out[...] = jnp.zeros_like(out)

    @pl.when((row < 2) & (col < 2) & (start < NB))
    def _():
        out[:, :NB] = low[pl.ds(pl.multiple_of(row * NB + start, B), mine), pl.ds(pl.multiple_of(col * NB, NB), NB)]


SMEM = pl.BlockSpec(memory_space=pltpu.SMEM)
VMEM = pl.BlockSpec(memory_space=pltpu.VMEM)


def call(kernel, outs, scratch, flops, *args):
    shape = lambda s: jax.ShapeDtypeStruct(s, F32)
    return pl.pallas_call(
        kernel,
        out_shape=tuple(shape(s) for s in outs),
        in_specs=[VMEM if v.ndim > 1 else SMEM for v in args],
        out_specs=(VMEM,) * len(outs),
        scratch_shapes=[pltpu.VMEM(s, F32) for s in scratch],
        compiler_params=pltpu.CompilerParams(vmem_limit_bytes=16 << 20),
        cost_estimate=pl.CostEstimate(flops=flops, bytes_accessed=1 << 20, transcendentals=0),
    )(*args)


def update(place, a, left, solved, low, rows):
    n, m = a.shape
    mine = 128
    block = lambda width: pl.BlockSpec((mine, width), lambda i: (i, 0))
    whole = lambda value: pl.BlockSpec(value.shape, lambda i: (0,) * value.ndim)
    return pl.pallas_call(
        update_kernel,
        grid=(n // mine,),
        out_shape=jax.ShapeDtypeStruct(a.shape, F32),
        in_specs=[SMEM, block(m), block(PANEL), block(PANEL), whole(low)] + [whole(v) for v in rows],
        out_specs=block(m),
        scratch_shapes=[pltpu.VMEM((PANEL, m), jnp.bfloat16)] * 2,
        compiler_params=pltpu.CompilerParams(vmem_limit_bytes=16 << 20),
        cost_estimate=pl.CostEstimate(flops=6 * n * m * PANEL, bytes_accessed=12 * n * m, transcendentals=0),
    )(place, a, left, solved, low, *rows)


def on_device(matrix):
    row, col = lax.axis_index("row"), lax.axis_index("col")
    x_index, core = row % NX, col % NK
    place = jnp.stack([row, col, x_index, core]).astype(jnp.int32)
    n = matrix.shape[0]
    half = matrix.shape[1] // 2
    full, block, tall, across, side = (PANEL, PANEL), (B, B), (2 * B, B), (B, PANEL), (n, PANEL)
    cost = 1_500_000_000

    sent = send(matrix[:NB, half:], along_x({0: 3, 1: 2}, lambda z, y, k: z == 0))
    quarter = lambda sent: jnp.where(row < NX, jnp.where(x_index < 2, matrix[:NB, :half], sent), 0.0)
    piece, corner, quarter = corner_tree(corner_piece(matrix[:NB, :NB], row, col), quarter, sent, x_index, core)
    left = jnp.where(col < NK, after(matrix[:, :NB], piece), 0.0)
    left = spread(left, [along_y(h) for h in HOPS[0]])

    quarter, left = pin((quarter, left), corner[0])
    corner = pin(corner, quarter, left)
    beside = send(quarter, along_x({i: i ^ 1 for i in range(NX)}))
    aside = send(quarter, along_x({i: i ^ 3 for i in range(NX)}))
    left = spread(left, [along_y(h) for h in HOPS[1]])
    state = call(first_kernel, [full] * 3, [tall, block], cost, place, *corner)
    state = call(functools.partial(next_kernel, 1), [full] * 3, [tall, block, across], cost, *state)
    beside, left = pin((beside, left), state[0])
    state = pin(state, beside, aside, left)
    opposite = send(beside, along_x({i: i ^ 3 for i in range(NX)}))
    other = send(left, other_core)
    state = call(functools.partial(next_kernel, 2), [full] * 3, [tall, block, across], cost, *state)
    low, solved, own = call(
        finish_kernel, [full, side, side], [full, side, tall, block, across], cost, place, left, other, *state
    )
    return update(place, matrix, own, solved, low, (quarter, beside, aside, opposite))


def solution(mesh):
    return jax.shard_map(on_device, mesh=mesh, in_specs=(P("row", "col"),), out_specs=P("row", "col"), check_vma=False)
```

time: 130 us -> 111 us (0.85)
  the two profiles are of different devices: /device:TPU:24 before, /device:TPU:88 now
where the time goes in v2:
time: 111 us; the launch traced here: 110 us
  starting transfers between devices  40.8 us (37%)
  waiting for transfers between devices  39.4 us (35%)
  Pallas kernels  24.4 us (22%)
  other arithmetic  4.04 us (4%)
  local copies, waits for them, and re-layouts  1.26 us (1%)
    ppermute x25, starting transfers between devices, send(): return lax.ppermute(value, BOTH, pairs)  40.8 us
    ppermute x25, waiting for transfers between devices, send(): return lax.ppermute(value, BOTH, pairs)  39.4 us
    pallas_call x4, Pallas kernels, call(): pl.pallas_call(kernel, out_shape=tuple((shape(s) for s in outs)), in_spec...  20.1 us
    pallas_call x1, Pallas kernels, update(): pl.pallas_call(update_kernel, grid=(n // mine,), out_shape=jax.ShapeDtype...  4.37 us
    add x8, other arithmetic, spread(): return functools.reduce(jnp.add, got, value)  2.78 us
  transfers between devices with their start and end apart: 25, of which 7 were waited for; matrix products, arithmetic and copies ran while one was open for 4% of the time, Pallas kernels for 18%

profile of v2, /device:TPU:88, one launch (start us, length us, event | category | flops | bytes accessed | tf_op | source)
XLA Modules:
  0.0 110.4 jit_solution(18161270165254825110)
XLA Ops:
  0.0 1.2 %slice.26 = f32[256,512]{1,0:T(8,128)S(1)} slice(f32[512,1024]{1,0:T(8,128)} %a.1), slice={[0:256], [512:1024]} | slice | bytes 1048576 | tf_op jit(solution)/shard_map/slice | solution.py:371
  1.2 1.5 %collective-permute-start = (f32[256,512]{1,0:T(8,128)S(1)}, f32[256,512]{1,0:T(8,128)}, u32[]{:S(2)}, u32[]{:S(2)}) collective-permute-start(f32[256,512]{1,0:T(8,128)S(1)} %slice.26), channel_id=1, source_target_pairs={{0,48},{1,49},{2,50},{3,51},{4,52},{5,53},{6,54},{7,55},{8,56},{9,... | collective-permute-start | bytes 1572872 | tf_op jit(solution)/shard_map/ppermute | solution.py:37
  2.7 0.9 select_select_fusion.3
  6.6 1.5 %collective-permute-start.2 = (f32[256,512]{1,0:T(8,128)S(1)}, f32[256,512]{1,0:T(8,128)}, u32[]{:S(2)}, u32[]{:S(2)}) collective-permute-start(f32[256,512]{1,0:T(8,128)S(1)} %select_select_fusion), channel_id=1, source_target_pairs={{0,320},{1,321},{2,322},{3,323},{4,324},{5,325},{6,326},{7,327},{8... | collective-permute-start | bytes 1572872 | tf_op jit(solution)/shard_map/ppermute | solution.py:37
  8.1 1.5 %collective-permute-start.1 = (f32[256,512]{1,0:T(8,128)S(1)}, f32[256,512]{1,0:T(8,128)}, u32[]{:S(2)}, u32[]{:S(2)}) collective-permute-start(f32[256,512]{1,0:T(8,128)S(1)} %select_select_fusion), channel_id=1, source_target_pairs={{0,192},{1,193},{2,194},{3,195},{4,196},{5,197},{6,198},{7,199},{8... | collective-permute-start | bytes 1572872 | tf_op jit(solution)/shard_map/ppermute | solution.py:37
  10.3 1.3 %collective-permute-start.9 = (f32[384,128]{1,0:T(8,128)S(1)}, f32[384,128]{1,0:T(8,128)}, u32[]{:S(2)}, u32[]{:S(2)}) collective-permute-start(f32[384,128]{1,0:T(8,128)S(1)} %add_add_fusion.6), channel_id=1, source_target_pairs={{0,6},{1,7},{16,22},{17,23},{64,70},{65,71},{80,86},{81,87},{128,1... | collective-permute-start | bytes 589832 | tf_op jit(solution)/shard_map/ppermute | solution.py:37
  11.7 21.3 %collective-permute-done.9 = f32[384,128]{1,0:T(8,128)} collective-permute-done((f32[384,128]{1,0:T(8,128)S(1)}, f32[384,128]{1,0:T(8,128)}, u32[]{:S(2)}, u32[]{:S(2)}) %collective-permute-start.9) | collective-permute-done | bytes 196640 | tf_op jit(solution)/shard_map/ppermute | solution.py:37
  33.0 1.0 add_add_fusion.5
  33.9 1.3 %collective-permute-start.12 = (f32[384,128]{1,0:T(8,128)S(1)}, f32[384,128]{1,0:T(8,128)S(1)}, u32[]{:S(2)}, u32[]{:S(2)}) collective-permute-start(f32[384,128]{1,0:T(8,128)S(1)} %add_add_fusion.5), channel_id=1, source_target_pairs={{0,14},{1,15},{6,4},{7,5},{16,30},{17,31},{22,20},{23,21},{64,78},... | collective-permute-start | bytes 589832 | tf_op jit(solution)/shard_map/ppermute | solution.py:37
  35.2 1.3 %collective-permute-start.11 = (f32[384,128]{1,0:T(8,128)S(1)}, f32[384,128]{1,0:T(8,128)S(1)}, u32[]{:S(2)}, u32[]{:S(2)}) collective-permute-start(f32[384,128]{1,0:T(8,128)S(1)} %add_add_fusion.5), channel_id=1, source_target_pairs={{0,2},{1,3},{6,8},{7,9},{10,12},{11,13},{16,18},{17,19},{22,24},{2... | collective-permute-start | bytes 589832 | tf_op jit(solution)/shard_map/ppermute | solution.py:37
  36.6 1.3 %add_add_fusion.3 = f32[256,512]{1,0:T(8,128)S(1)} fusion(f32[256,512]{1,0:T(8,128)} %collective-permute-done.2, f32[256,512]{1,0:T(8,128)S(1)} %select_select_fusion, f32[256,512]{1,0:T(8,128)} %collective-permute-done.1), kind=kLoop, calls=%fused_computation.3 | loop fusion | flops 262144 | bytes 2097152 | tf_op jit(solution)/shard_map/add | solution.py:63
  37.9 1.8 %collective-permute-done.11 = f32[384,128]{1,0:T(8,128)S(1)} collective-permute-done((f32[384,128]{1,0:T(8,128)S(1)}, f32[384,128]{1,0:T(8,128)S(1)}, u32[]{:S(2)}, u32[]{:S(2)}) %collective-permute-start.11) | collective-permute-done | bytes 196640 | tf_op jit(solution)/shard_map/ppermute | solution.py:37
  39.7 3.4 %collective-permute-start.17 = (f32[384,128]{1,0:T(8,128)S(1)}, f32[384,128]{1,0:T(8,128)S(1)}, u32[]{:S(2)}, u32[]{:S(2)}) collective-permute-start(f32[384,128]{1,0:T(8,128)S(1)} %add_add_fusion.4), channel_id=1, source_target_pairs={{0,16},{1,17},{2,18},{3,19},{4,20},{5,21},{6,22},{7,23},{8,24},{9,... | collective-permute-start | bytes 589832 | tf_op jit(solution)/shard_map/ppermute | solution.py:37
  43.1 1.3 %collective-permute-start.16 = (f32[384,128]{1,0:T(8,128)S(1)}, f32[384,128]{1,0:T(8,128)S(1)}, u32[]{:S(2)}, u32[]{:S(2)}) collective-permute-start(f32[384,128]{1,0:T(8,128)S(1)} %add_add_fusion.4), channel_id=1, source_target_pairs={{0,32},{1,33},{2,34},{3,35},{4,36},{5,37},{6,38},{7,39},{8,40},{9,... | collective-permute-start | bytes 589832 | tf_op jit(solution)/shard_map/ppermute | solution.py:37
  44.4 1.3 %collective-permute-start.15 = (f32[384,128]{1,0:T(8,128)S(1)}, f32[384,128]{1,0:T(8,128)S(1)}, u32[]{:S(2)}, u32[]{:S(2)}) collective-permute-start(f32[384,128]{1,0:T(8,128)S(1)} %add_add_fusion.4), channel_id=1, source_target_pairs={{0,48},{1,49},{2,50},{3,51},{4,52},{5,53},{6,54},{7,55},{8,56},{9,... | collective-permute-start | bytes 589832 | tf_op jit(solution)/shard_map/ppermute | solution.py:37
  46.5 1.3 %collective-permute-start.13 = (f32[512,256]{1,0:T(8,128)S(1)}, f32[512,256]{1,0:T(8,128)S(1)}, u32[]{:S(2)}, u32[]{:S(2)}) collective-permute-start(f32[512,256]{1,0:T(8,128)S(1)} %broadcast_select_fusion), channel_id=1, source_target_pairs={{0,6},{1,7},{16,22},{17,23},{32,38},{33,39},{48,54},{49,55},{64,70... | collective-permute-start | bytes 1572872 | tf_op jit(solution)/shard_map/ppermute | solution.py:37
  48.6 1.3 %collective-permute-start.3 = (f32[256,512]{1,0:T(8,128)S(1)}, f32[256,512]{1,0:T(8,128)S(1)}, u32[]{:S(2)}, u32[]{:S(2)}) collective-permute-start(f32[256,512]{1,0:T(8,128)S(1)} %add_add_fusion.3), channel_id=1, source_target_pairs={{0,64},{1,65},{2,66},{3,67},{4,68},{5,69},{6,70},{7,71},{8,72},{9,... | collective-permute-start | bytes 1572872 | tf_op jit(solution)/shard_map/ppermute | solution.py:37
  50.7 1.9 %collective-permute-start.21 = (f32[640,128]{1,0:T(8,128)S(1)}, f32[640,128]{1,0:T(8,128)S(1)}, u32[]{:S(2)}, u32[]{:S(2)}) collective-permute-start(f32[640,128]{1,0:T(8,128)S(1)} %pad_maximum_fusion.own), channel_id=1, source_target_pairs={{0,1},{1,0},{2,3},{3,2},{4,5},{5,4},{6,7},{7,6},{8,9},{9,8},{10,11... | collective-permute-start | bytes 983048 | tf_op jit(solution)/shard_map/ppermute | solution.py:37
  52.7 8.0 %collective-permute-done.13 = f32[512,256]{1,0:T(8,128)S(1)} collective-permute-done((f32[512,256]{1,0:T(8,128)S(1)}, f32[512,256]{1,0:T(8,128)S(1)}, u32[]{:S(2)}, u32[]{:S(2)}) %collective-permute-start.13) | collective-permute-done | bytes 524320 | tf_op jit(solution)/shard_map/ppermute | solution.py:37
  60.7 3.7 %collective-permute-done.3 = f32[256,512]{1,0:T(8,128)S(1)} collective-permute-done((f32[256,512]{1,0:T(8,128)S(1)}, f32[256,512]{1,0:T(8,128)S(1)}, u32[]{:S(2)}, u32[]{:S(2)}) %collective-permute-start.3) | collective-permute-done | bytes 524320 | tf_op jit(solution)/shard_map/ppermute | solution.py:37
  64.6 2.2 %collective-permute-start.20 = (f32[512,256]{1,0:T(8,128)S(1)}, f32[512,256]{1,0:T(8,128)S(1)}, u32[]{:S(2)}, u32[]{:S(2)}) collective-permute-start(f32[512,256]{1,0:T(8,128)S(1)} %add_add_fusion.1), channel_id=1, source_target_pairs={{0,14},{1,15},{6,4},{7,5},{16,30},{17,31},{22,20},{23,21},{32,46},... | collective-permute-start | bytes 1572872 | tf_op jit(solution)/shard_map/ppermute | solution.py:37
  66.8 3.2 %collective-permute-start.19 = (f32[512,256]{1,0:T(8,128)S(1)}, f32[512,256]{1,0:T(8,128)S(1)}, u32[]{:S(2)}, u32[]{:S(2)}) collective-permute-start(f32[512,256]{1,0:T(8,128)S(1)} %add_add_fusion.1), channel_id=1, source_target_pairs={{0,2},{1,3},{6,8},{7,9},{10,12},{11,13},{16,18},{17,19},{22,24},{2... | collective-permute-start | bytes 1572872 | tf_op jit(solution)/shard_map/ppermute | solution.py:37
  70.1 4.9 %collective-permute-start.23 = (f32[256,512]{1,0:T(8,128)S(1)}, f32[256,512]{1,0:T(8,128)S(1)}, u32[]{:S(2)}, u32[]{:S(2)}) collective-permute-start(f32[256,512]{1,0:T(8,128)S(1)} %add_add_fusion.2.here), channel_id=1, source_target_pairs={{0,48},{1,49},{2,50},{3,51},{4,52},{5,53},{6,54},{7,55},{8,56},{9,... | collective-permute-start | bytes 1572872 | tf_op jit(solution)/shard_map/ppermute | solution.py:37
  75.0 2.3 %collective-permute-start.18 = (f32[256,512]{1,0:T(8,128)S(1)}, f32[256,512]{1,0:T(8,128)S(1)}, u32[]{:S(2)}, u32[]{:S(2)}) collective-permute-start(f32[256,512]{1,0:T(8,128)S(1)} %add_add_fusion.2.here), channel_id=1, source_target_pairs={{0,16},{1,17},{2,18},{3,19},{4,20},{5,21},{6,22},{7,23},{8,24},{9,... | collective-permute-start | bytes 1572872 | tf_op jit(solution)/shard_map/ppermute | solution.py:37
  77.3 4.8 %shard_map.17 = (f32[512,512]{1,0:T(8,128)S(1)}, f32[512,512]{1,0:T(8,128)S(1)}, f32[512,512]{1,0:T(8,128)S(1)}) custom-call(s32[4]{0:T(128)S(1)} %pad_add_fusion.place, f32[640,128]{1,0:T(8,128)S(1)} %pad_maximum_fusion.own, f32[640,128]{1,0:T(8,128)S(1)} %collective-permute-done.21.other), custom_call_target="tpu_custom_call" | custom-call | flops 1500000000 | bytes 1048576 | tf_op jit(solution)/shard_map/pallas_call | solution.py:334
  82.2 4.4 %shard_map.18 = (f32[512,512]{1,0:T(8,128)S(1)}, f32[512,512]{1,0:T(8,128)S(1)}, f32[512,512]{1,0:T(8,128)S(1)}) custom-call(f32[512,512]{1,0:T(8,128)S(1)} %get-tuple-element.36.low_in, f32[512,512]{1,0:T(8,128)S(1)} %get-tuple-element.37.inv_in, f32[512,512]{1,0:T(8,128)S(1)} %get-tuple-element.38.a_in), custom_call_target="tpu_custom_call" | custom-call | flops 1500000000 | bytes 1048576 | tf_op jit(solution)/shard_map/pallas_call | solution.py:334
  86.7 1.9 %collective-permute-start.22 = (f32[512,256]{1,0:T(8,128)S(1)}, f32[512,256]{1,0:T(8,128)S(1)}, u32[]{:S(2)}, u32[]{:S(2)}) collective-permute-start(f32[512,256]{1,0:T(8,128)S(1)} %add_add_fusion.own), channel_id=1, source_target_pairs={{0,1},{1,0},{2,3},{3,2},{4,5},{5,4},{6,7},{7,6},{8,9},{9,8},{10,11... | collective-permute-start | bytes 1572872 | tf_op jit(solution)/shard_map/ppermute | solution.py:37
  88.6 2.7 %collective-permute-start.24 = (f32[256,512]{1,0:T(8,128)S(1)}, f32[256,512]{1,0:T(8,128)S(1)}, u32[]{:S(2)}, u32[]{:S(2)}) collective-permute-start(f32[256,512]{1,0:T(8,128)S(1)} %collective-permute-done.18.beside), channel_id=1, source_target_pairs={{0,48},{1,49},{2,50},{3,51},{4,52},{5,53},{6,54},{7,55},{8,56},{9,... | collective-permute-start | bytes 1572872 | tf_op jit(solution)/shard_map/ppermute | solution.py:37
  91.4 4.4 %shard_map.19 = (f32[512,512]{1,0:T(8,128)S(1)}, f32[512,512]{1,0:T(8,128)S(1)}, f32[512,512]{1,0:T(8,128)S(1)}) custom-call(f32[512,512]{1,0:T(8,128)S(1)} %get-tuple-element.44.low_in, f32[512,512]{1,0:T(8,128)S(1)} %get-tuple-element.45.inv_in, f32[512,512]{1,0:T(8,128)S(1)} %get-tuple-element.46.a_in), custom_call_target="tpu_custom_call" | custom-call | flops 1500000000 | bytes 1048576 | tf_op jit(solution)/shard_map/pallas_call | solution.py:334
  95.8 6.4 %shard_map.20 = (f32[512,512]{1,0:T(8,128)S(1)}, f32[512,512]{1,0:T(8,128)S(1)}, f32[512,512]{1,0:T(8,128)S(1)}) custom-call(s32[4]{0:T(128)S(1)} %pad_add_fusion.place, f32[512,256]{1,0:T(8,128)S(1)} %add_add_fusion.own, f32[512,256]{1,0:T(8,128)S(1)} %collective-permute-done.22.other, f32[512,512]{1,0:T(8,128)S(1)} %get-tuple-element.47.low_in, ...), custom_call_target="tpu_custom_call" | custom-call | flops 1500000000 | bytes 1048576 | tf_op jit(solution)/shard_map/pallas_call | solution.py:334
  102.2 3.9 %collective-permute-done.24.opposite = f32[256,512]{1,0:T(8,128)S(1)} collective-permute-done((f32[256,512]{1,0:T(8,128)S(1)}, f32[256,512]{1,0:T(8,128)S(1)}, u32[]{:S(2)}, u32[]{:S(2)}) %collective-permute-start.24) | collective-permute-done | bytes 524320 | tf_op jit(solution)/shard_map/ppermute | solution.py:37
  106.1 4.4 %shard_map.21 = f32[512,1024]{1,0:T(8,128)} custom-call(s32[4]{0:T(128)S(1)} %pad_add_fusion.place, f32[512,1024]{1,0:T(8,128)S(1)} %copy-done, f32[512,512]{1,0:T(8,128)S(1)} %get-tuple-element.50.left, f32[512,512]{1,0:T(8,128)S(1)} %get-tuple-element.51.solved, f32[512,512]{1,0:T(8,128)S(1)} %get-tuple-element.52.low, f32[256,512]{1,0:T(8,128)S(1)} %add_add_fusion.2.here, ...), custom_call_target="tpu_custom_call" | custom-call | flops 1610612736 | bytes 6291456 | tf_op jit(solution)/shard_map/pallas_call | solution.py:350
  (43 shorter events, 6.5 us)
Async XLA Ops:
  0.0 6.5 %copy-start = (f32[512,1024]{1,0:T(8,128)S(1)}, f32[512,1024]{1,0:T(8,128)}, u32[]{:S(2)}) copy-start(f32[512,1024]{1,0:T(8,128)} %a.1) | copy-start | bytes 6291460
  1.2 5.2 %collective-permute-start = (f32[256,512]{1,0:T(8,128)S(1)}, f32[256,512]{1,0:T(8,128)}, u32[]{:S(2)}, u32[]{:S(2)}) collective-permute-start(f32[256,512]{1,0:T(8,128)S(1)} %slice.26), channel_id=1, source_target_pairs={{0,48},{1,49},{2,50},{3,51},{4,52},{5,53},{6,54},{7,55},{8,56},{9,... | collective-permute-start | bytes 1572872 | tf_op jit(solution)/shard_map/ppermute | solution.py:37
  3.7 1.4 %collective-permute-start.6 = (f32[384,128]{1,0:T(8,128)S(1)}, f32[384,128]{1,0:T(8,128)S(1)}, u32[]{:S(2)}, u32[]{:S(2)}) collective-permute-start(f32[384,128]{1,0:T(8,128)S(1)} %maximum_select_fusion), channel_id=1, source_target_pairs={{0,320},{1,321},{16,336},{17,337}} | collective-permute-start | bytes 589832 | tf_op jit(solution)/shard_map/ppermute | solution.py:37
  4.3 0.7 collective-permute-start.5
  5.1 4.5 %collective-permute-start.8 = (f32[384,128]{1,0:T(8,128)S(1)}, f32[384,128]{1,0:T(8,128)S(1)}, u32[]{:S(2)}, u32[]{:S(2)}) collective-permute-start(f32[384,128]{1,0:T(8,128)S(1)} %add_add_fusion.7), channel_id=1, source_target_pairs={{0,448},{1,449},{16,464},{17,465},{192,128},{193,129},{208,144},{2... | collective-permute-start | bytes 589832 | tf_op jit(solution)/shard_map/ppermute | solution.py:37
  5.8 3.8 %collective-permute-start.7 = (f32[384,128]{1,0:T(8,128)S(1)}, f32[384,128]{1,0:T(8,128)S(1)}, u32[]{:S(2)}, u32[]{:S(2)}) collective-permute-start(f32[384,128]{1,0:T(8,128)S(1)} %add_add_fusion.7), channel_id=1, source_target_pairs={{0,64},{1,65},{16,80},{17,81},{192,256},{193,257},{208,272},{209,2... | collective-permute-start | bytes 589832 | tf_op jit(solution)/shard_map/ppermute | solution.py:37
  6.6 29.9 %collective-permute-start.2 = (f32[256,512]{1,0:T(8,128)S(1)}, f32[256,512]{1,0:T(8,128)}, u32[]{:S(2)}, u32[]{:S(2)}) collective-permute-start(f32[256,512]{1,0:T(8,128)S(1)} %select_select_fusion), channel_id=1, source_target_pairs={{0,320},{1,321},{2,322},{3,323},{4,324},{5,325},{6,326},{7,327},{8... | collective-permute-start | bytes 1572872 | tf_op jit(solution)/shard_map/ppermute | solution.py:37
  8.1 28.5 %collective-permute-start.1 = (f32[256,512]{1,0:T(8,128)S(1)}, f32[256,512]{1,0:T(8,128)}, u32[]{:S(2)}, u32[]{:S(2)}) collective-permute-start(f32[256,512]{1,0:T(8,128)S(1)} %select_select_fusion), channel_id=1, source_target_pairs={{0,192},{1,193},{2,194},{3,195},{4,196},{5,197},{6,198},{7,199},{8... | collective-permute-start | bytes 1572872 | tf_op jit(solution)/shard_map/ppermute | solution.py:37
  9.6 2.1 %collective-permute-start.10 = (f32[384,128]{1,0:T(8,128)S(1)}, f32[384,128]{1,0:T(8,128)S(1)}, u32[]{:S(2)}, u32[]{:S(2)}) collective-permute-start(f32[384,128]{1,0:T(8,128)S(1)} %add_add_fusion.6), channel_id=1, source_target_pairs={{0,10},{1,11},{16,26},{17,27},{64,74},{65,75},{80,90},{81,91},{128... | collective-permute-start | bytes 589832 | tf_op jit(solution)/shard_map/ppermute | solution.py:37
  10.3 22.7 %collective-permute-start.9 = (f32[384,128]{1,0:T(8,128)S(1)}, f32[384,128]{1,0:T(8,128)}, u32[]{:S(2)}, u32[]{:S(2)}) collective-permute-start(f32[384,128]{1,0:T(8,128)S(1)} %add_add_fusion.6), channel_id=1, source_target_pairs={{0,6},{1,7},{16,22},{17,23},{64,70},{65,71},{80,86},{81,87},{128,1... | collective-permute-start | bytes 589832 | tf_op jit(solution)/shard_map/ppermute | solution.py:37
  33.9 5.8 %collective-permute-start.12 = (f32[384,128]{1,0:T(8,128)S(1)}, f32[384,128]{1,0:T(8,128)S(1)}, u32[]{:S(2)}, u32[]{:S(2)}) collective-permute-start(f32[384,128]{1,0:T(8,128)S(1)} %add_add_fusion.5), channel_id=1, source_target_pairs={{0,14},{1,15},{6,4},{7,5},{16,30},{17,31},{22,20},{23,21},{64,78},... | collective-permute-start | bytes 589832 | tf_op jit(solution)/shard_map/ppermute | solution.py:37
  35.2 4.5 %collective-permute-start.11 = (f32[384,128]{1,0:T(8,128)S(1)}, f32[384,128]{1,0:T(8,128)S(1)}, u32[]{:S(2)}, u32[]{:S(2)}) collective-permute-start(f32[384,128]{1,0:T(8,128)S(1)} %add_add_fusion.5), channel_id=1, source_target_pairs={{0,2},{1,3},{6,8},{7,9},{10,12},{11,13},{16,18},{17,19},{22,24},{2... | collective-permute-start | bytes 589832 | tf_op jit(solution)/shard_map/ppermute | solution.py:37
  39.7 8.1 %collective-permute-start.17 = (f32[384,128]{1,0:T(8,128)S(1)}, f32[384,128]{1,0:T(8,128)S(1)}, u32[]{:S(2)}, u32[]{:S(2)}) collective-permute-start(f32[384,128]{1,0:T(8,128)S(1)} %add_add_fusion.4), channel_id=1, source_target_pairs={{0,16},{1,17},{2,18},{3,19},{4,20},{5,21},{6,22},{7,23},{8,24},{9,... | collective-permute-start | bytes 589832 | tf_op jit(solution)/shard_map/ppermute | solution.py:37
  43.1 5.5 %collective-permute-start.16 = (f32[384,128]{1,0:T(8,128)S(1)}, f32[384,128]{1,0:T(8,128)S(1)}, u32[]{:S(2)}, u32[]{:S(2)}) collective-permute-start(f32[384,128]{1,0:T(8,128)S(1)} %add_add_fusion.4), channel_id=1, source_target_pairs={{0,32},{1,33},{2,34},{3,35},{4,36},{5,37},{6,38},{7,39},{8,40},{9,... | collective-permute-start | bytes 589832 | tf_op jit(solution)/shard_map/ppermute | solution.py:37
  44.4 6.2 %collective-permute-start.15 = (f32[384,128]{1,0:T(8,128)S(1)}, f32[384,128]{1,0:T(8,128)S(1)}, u32[]{:S(2)}, u32[]{:S(2)}) collective-permute-start(f32[384,128]{1,0:T(8,128)S(1)} %add_add_fusion.4), channel_id=1, source_target_pairs={{0,48},{1,49},{2,50},{3,51},{4,52},{5,53},{6,54},{7,55},{8,56},{9,... | collective-permute-start | bytes 589832 | tf_op jit(solution)/shard_map/ppermute | solution.py:37
  45.8 6.9 %collective-permute-start.14 = (f32[512,256]{1,0:T(8,128)S(1)}, f32[512,256]{1,0:T(8,128)S(1)}, u32[]{:S(2)}, u32[]{:S(2)}) collective-permute-start(f32[512,256]{1,0:T(8,128)S(1)} %broadcast_select_fusion), channel_id=1, source_target_pairs={{0,10},{1,11},{16,26},{17,27},{32,42},{33,43},{48,58},{49,59},{64,... | collective-permute-start | bytes 1572872 | tf_op jit(solution)/shard_map/ppermute | solution.py:37
  46.5 14.1 %collective-permute-start.13 = (f32[512,256]{1,0:T(8,128)S(1)}, f32[512,256]{1,0:T(8,128)S(1)}, u32[]{:S(2)}, u32[]{:S(2)}) collective-permute-start(f32[512,256]{1,0:T(8,128)S(1)} %broadcast_select_fusion), channel_id=1, source_target_pairs={{0,6},{1,7},{16,22},{17,23},{32,38},{33,39},{48,54},{49,55},{64,70... | collective-permute-start | bytes 1572872 | tf_op jit(solution)/shard_map/ppermute | solution.py:37
  47.8 12.9 %collective-permute-start.4 = (f32[256,512]{1,0:T(8,128)S(1)}, f32[256,512]{1,0:T(8,128)S(1)}, u32[]{:S(2)}, u32[]{:S(2)}) collective-permute-start(f32[256,512]{1,0:T(8,128)S(1)} %add_add_fusion.3), channel_id=1, source_target_pairs={{0,448},{1,449},{2,450},{3,451},{4,452},{5,453},{6,454},{7,455},{8... | collective-permute-start | bytes 1572872 | tf_op jit(solution)/shard_map/ppermute | solution.py:37
  48.6 15.8 %collective-permute-start.3 = (f32[256,512]{1,0:T(8,128)S(1)}, f32[256,512]{1,0:T(8,128)S(1)}, u32[]{:S(2)}, u32[]{:S(2)}) collective-permute-start(f32[256,512]{1,0:T(8,128)S(1)} %add_add_fusion.3), channel_id=1, source_target_pairs={{0,64},{1,65},{2,66},{3,67},{4,68},{5,69},{6,70},{7,71},{8,72},{9,... | collective-permute-start | bytes 1572872 | tf_op jit(solution)/shard_map/ppermute | solution.py:37
  50.7 26.6 %collective-permute-start.21 = (f32[640,128]{1,0:T(8,128)S(1)}, f32[640,128]{1,0:T(8,128)S(1)}, u32[]{:S(2)}, u32[]{:S(2)}) collective-permute-start(f32[640,128]{1,0:T(8,128)S(1)} %pad_maximum_fusion.own), channel_id=1, source_target_pairs={{0,1},{1,0},{2,3},{3,2},{4,5},{5,4},{6,7},{7,6},{8,9},{9,8},{10,11... | collective-permute-start | bytes 983048 | tf_op jit(solution)/shard_map/ppermute | solution.py:37
  64.6 22.0 %collective-permute-start.20 = (f32[512,256]{1,0:T(8,128)S(1)}, f32[512,256]{1,0:T(8,128)S(1)}, u32[]{:S(2)}, u32[]{:S(2)}) collective-permute-start(f32[512,256]{1,0:T(8,128)S(1)} %add_add_fusion.1), channel_id=1, source_target_pairs={{0,14},{1,15},{6,4},{7,5},{16,30},{17,31},{22,20},{23,21},{32,46},... | collective-permute-start | bytes 1572872 | tf_op jit(solution)/shard_map/ppermute | solution.py:37
  66.8 19.8 %collective-permute-start.19 = (f32[512,256]{1,0:T(8,128)S(1)}, f32[512,256]{1,0:T(8,128)S(1)}, u32[]{:S(2)}, u32[]{:S(2)}) collective-permute-start(f32[512,256]{1,0:T(8,128)S(1)} %add_add_fusion.1), channel_id=1, source_target_pairs={{0,2},{1,3},{6,8},{7,9},{10,12},{11,13},{16,18},{17,19},{22,24},{2... | collective-permute-start | bytes 1572872 | tf_op jit(solution)/shard_map/ppermute | solution.py:37
  70.1 21.2 %collective-permute-start.23 = (f32[256,512]{1,0:T(8,128)S(1)}, f32[256,512]{1,0:T(8,128)S(1)}, u32[]{:S(2)}, u32[]{:S(2)}) collective-permute-start(f32[256,512]{1,0:T(8,128)S(1)} %add_add_fusion.2.here), channel_id=1, source_target_pairs={{0,48},{1,49},{2,50},{3,51},{4,52},{5,53},{6,54},{7,55},{8,56},{9,... | collective-permute-start | bytes 1572872 | tf_op jit(solution)/shard_map/ppermute | solution.py:37
  75.0 11.7 %collective-permute-start.18 = (f32[256,512]{1,0:T(8,128)S(1)}, f32[256,512]{1,0:T(8,128)S(1)}, u32[]{:S(2)}, u32[]{:S(2)}) collective-permute-start(f32[256,512]{1,0:T(8,128)S(1)} %add_add_fusion.2.here), channel_id=1, source_target_pairs={{0,16},{1,17},{2,18},{3,19},{4,20},{5,21},{6,22},{7,23},{8,24},{9,... | collective-permute-start | bytes 1572872 | tf_op jit(solution)/shard_map/ppermute | solution.py:37
  86.7 9.0 %collective-permute-start.22 = (f32[512,256]{1,0:T(8,128)S(1)}, f32[512,256]{1,0:T(8,128)S(1)}, u32[]{:S(2)}, u32[]{:S(2)}) collective-permute-start(f32[512,256]{1,0:T(8,128)S(1)} %add_add_fusion.own), channel_id=1, source_target_pairs={{0,1},{1,0},{2,3},{3,2},{4,5},{5,4},{6,7},{7,6},{8,9},{9,8},{10,11... | collective-permute-start | bytes 1572872 | tf_op jit(solution)/shard_map/ppermute | solution.py:37
  88.6 17.4 %collective-permute-start.24 = (f32[256,512]{1,0:T(8,128)S(1)}, f32[256,512]{1,0:T(8,128)S(1)}, u32[]{:S(2)}, u32[]{:S(2)}) collective-permute-start(f32[256,512]{1,0:T(8,128)S(1)} %collective-permute-done.18.beside), channel_id=1, source_target_pairs={{0,48},{1,49},{2,50},{3,51},{4,52},{5,53},{6,54},{7,55},{8,56},{9,... | collective-permute-start | bytes 1572872 | tf_op jit(solution)/shard_map/ppermute | solution.py:37

commit v3 on v2

--- a/solution.py
+++ b/solution.py
@@ -167,6 +167,17 @@
     return pl.ds(i * B, B), pl.ds(j * B, B)
 
 
+def split(value):
+    high = value.astype(jnp.bfloat16)
+    return high, (value - high.astype(F32)).astype(jnp.bfloat16)
+
+
+def product(a, b, dims):
+    one = lambda u, v: lax.dot_general(u, v, (dims, ((), ())), preferred_element_type=F32)
+    (ah, al), (bh, bl) = split(a), split(b)
+    return one(ah, bh) + (one(ah, bl) + one(al, bh))
+
+
 def outer(a, b):
     return dot(a, b, ((1,), (1,)))
 
@@ -216,7 +227,7 @@
         trail_task(a, low, i + 1, i + 1, i)()
 
 
-def first_kernel(place, own, other, low, inv, a, d, up):
+def first_kernel(place, own, other, low, inv, a, d, up, mid):
     first = place[3] == 0
     block = lambda ref, i: ref[i * B : (i + 1) * B, :]
     p0 = [jnp.where(first, block(own, i), block(other, i)) for i in range(5)]
@@ -231,20 +242,19 @@
     low[...] = jnp.zeros_like(low)
     inv[...] = jnp.zeros_like(inv)
     factor_step(0, low, inv, a, d, up, ())
-
-
-def next_kernel(i, low_in, inv_in, a_in, low, inv, a, d, up, mid):
+    tasks = [below_task(a, low, inv, m, 0) for m in (2, 3)]
+    tasks += [trail_task(a, low, m, n, 0) for m, n in ((2, 1), (2, 2), (3, 1), (3, 2), (3, 3))]
+    factor_step(1, low, inv, a, d, up, tasks + [gather_task(low, inv, mid, 1)])
+    invert_task(inv, mid, 1)()
+
+
+def next_kernel(low_in, inv_in, a_in, low, inv, a, d, up, mid):
     low[...] = low_in[...]
     inv[...] = inv_in[...]
     a[...] = a_in[...]
-    if i == 1:
-        tasks = [below_task(a, low, inv, m, 0) for m in (2, 3)]
-        tasks += [trail_task(a, low, m, n, 0) for m, n in ((2, 1), (2, 2), (3, 1), (3, 2), (3, 3))]
-        tasks += [gather_task(low, inv, mid, 1)]
-    else:
-        tasks = [below_task(a, low, inv, 3, 1), trail_task(a, low, 3, 2, 1), trail_task(a, low, 3, 3, 1), gather_task(low, inv, mid, 2)]
-    factor_step(i, low, inv, a, d, up, tasks)
-    invert_task(inv, mid, i)()
+    tasks = [below_task(a, low, inv, 3, 1), trail_task(a, low, 3, 2, 1), trail_task(a, low, 3, 3, 1), gather_task(low, inv, mid, 2)]
+    factor_step(2, low, inv, a, d, up, tasks)
+    invert_task(inv, mid, 2)()
 
 
 def finish_kernel(place, own, other, low_in, inv_in, a_in, low, solved, left, inv, p, d, up, mid):
@@ -253,24 +263,26 @@
     inv[...] = inv_in[...]
     p[:, :NB] = jnp.where(first, own[...], other[...])
     p[:, NB:] = jnp.where(first, other[...], own[...])
-    left[...] = jnp.zeros_like(left)
     cols = lambda j: (slice(None), pl.ds(j * B, B))
 
     def solve(j):
         def task():
-            solved[cols(j)] = outer(p[cols(j)], inv[at(j, j)])
+            solved[cols(j)] = product(p[cols(j)], inv[at(j, j)], ((1,), (1,)))
 
         return task
 
     def panel(i, j):
         def task():
-            p[cols(i)] = p[cols(i)] - outer(solved[cols(j)], low[at(i, j)])
+            p[cols(i)] = p[cols(i)] - product(solved[cols(j)], low[at(i, j)], ((1,), (1,)))
 
         return task
 
     def add(j):
         def task():
-            left[:, upto(j + 1)] = left[:, upto(j + 1)] + inner(solved[cols(j)], inv[pl.ds(j * B, B), upto(j + 1)])
+            term = product(solved[cols(j)], inv[pl.ds(j * B, B), upto(j + 1)], ((1,), (0,)))
+            if j:
+                left[:, upto(j)] = left[:, upto(j)] + term[:, : j * B]
+            left[cols(j)] = term[:, j * B :]
 
         return task
 
@@ -284,11 +296,6 @@
     solve(3)()
     invert_task(inv, mid, 3)()
     add(3)()
-
-
-def split(value):
-    high = value.astype(jnp.bfloat16)
-    return high, (value - high.astype(F32)).astype(jnp.bfloat16)
 
 
 def update_kernel(place, a, left, solved, low, here, beside, across, opposite, out, high, rest):
@@ -344,7 +351,7 @@
 
 def update(place, a, left, solved, low, rows):
     n, m = a.shape
-    mine = 128
+    mine = 256
     block = lambda width: pl.BlockSpec((mine, width), lambda i: (i, 0))
     whole = lambda value: pl.BlockSpec(value.shape, lambda i: (0,) * value.ndim)
     return pl.pallas_call(
@@ -379,13 +386,12 @@
     beside = send(quarter, along_x({i: i ^ 1 for i in range(NX)}))
     aside = send(quarter, along_x({i: i ^ 3 for i in range(NX)}))
     left = spread(left, [along_y(h) for h in HOPS[1]])
-    state = call(first_kernel, [full] * 3, [tall, block], cost, place, *corner)
-    state = call(functools.partial(next_kernel, 1), [full] * 3, [tall, block, across], cost, *state)
+    state = call(first_kernel, [full] * 3, [tall, block, across], 2 * cost, place, *corner)
     beside, left = pin((beside, left), state[0])
     state = pin(state, beside, aside, left)
     opposite = send(beside, along_x({i: i ^ 3 for i in range(NX)}))
     other = send(left, other_core)
-    state = call(functools.partial(next_kernel, 2), [full] * 3, [tall, block, across], cost, *state)
+    state = call(next_kernel, [full] * 3, [tall, block, across], cost, *state)
     low, solved, own = call(
         finish_kernel, [full, side, side], [full, side, tall, block, across], cost, place, left, other, *state
     )

time: 111 us -> 111 us (level)
  Pallas kernels: 24.4 us -> 22.9 us
    pallas_call x4 -> x3, Pallas kernels: 20.1 us -> 19 us  [call(): pl.pallas_call(kernel, out_shape=tuple((shape(s) for s in outs)), in_spec...]
  transfers between devices with their start and end apart: 25 -> 25, of which waited for: 7 -> 7; matrix products, arithmetic and copies ran while one was open for 4% -> 4% of each run, Pallas kernels for 18% -> 17%
where the time goes in v3:
time: 111 us; the launch traced here: 110 us
  starting transfers between devices  40.8 us (37%)
  waiting for transfers between devices  40.3 us (36%)
  Pallas kernels  22.9 us (21%)
  other arithmetic  4.03 us (4%)
  local copies, waits for them, and re-layouts  1.26 us (1%)
    ppermute x25, starting transfers between devices, send(): return lax.ppermute(value, BOTH, pairs)  40.8 us
    ppermute x25, waiting for transfers between devices, send(): return lax.ppermute(value, BOTH, pairs)  40.3 us
    pallas_call x3, Pallas kernels, call(): pl.pallas_call(kernel, out_shape=tuple((shape(s) for s in outs)), in_spec...  19 us
    pallas_call x1, Pallas kernels, update(): pl.pallas_call(update_kernel, grid=(n // mine,), out_shape=jax.ShapeDtype...  3.92 us
    add x8, other arithmetic, spread(): return functools.reduce(jnp.add, got, value)  2.77 us
  transfers between devices with their start and end apart: 25, of which 7 were waited for; matrix products, arithmetic and copies ran while one was open for 4% of the time, Pallas kernels for 17%

profile of v3, /device:TPU:88, one launch (start us, length us, event | category | flops | bytes accessed | tf_op | source)
XLA Modules:
  0.0 109.8 jit_solution(12302461889893418173)
XLA Ops:
  0.0 1.2 %slice.26 = f32[256,512]{1,0:T(8,128)S(1)} slice(f32[512,1024]{1,0:T(8,128)} %a.1), slice={[0:256], [512:1024]} | slice | bytes 1048576 | tf_op jit(solution)/shard_map/slice | solution.py:378
  1.2 1.5 %collective-permute-start = (f32[256,512]{1,0:T(8,128)S(1)}, f32[256,512]{1,0:T(8,128)}, u32[]{:S(2)}, u32[]{:S(2)}) collective-permute-start(f32[256,512]{1,0:T(8,128)S(1)} %slice.26), channel_id=1, source_target_pairs={{0,48},{1,49},{2,50},{3,51},{4,52},{5,53},{6,54},{7,55},{8,56},{9,... | collective-permute-start | bytes 1572872 | tf_op jit(solution)/shard_map/ppermute | solution.py:37
  2.7 0.9 select_select_fusion.3
  6.6 1.5 %collective-permute-start.2 = (f32[256,512]{1,0:T(8,128)S(1)}, f32[256,512]{1,0:T(8,128)}, u32[]{:S(2)}, u32[]{:S(2)}) collective-permute-start(f32[256,512]{1,0:T(8,128)S(1)} %select_select_fusion), channel_id=1, source_target_pairs={{0,320},{1,321},{2,322},{3,323},{4,324},{5,325},{6,326},{7,327},{8... | collective-permute-start | bytes 1572872 | tf_op jit(solution)/shard_map/ppermute | solution.py:37
  8.1 1.5 %collective-permute-start.1 = (f32[256,512]{1,0:T(8,128)S(1)}, f32[256,512]{1,0:T(8,128)}, u32[]{:S(2)}, u32[]{:S(2)}) collective-permute-start(f32[256,512]{1,0:T(8,128)S(1)} %select_select_fusion), channel_id=1, source_target_pairs={{0,192},{1,193},{2,194},{3,195},{4,196},{5,197},{6,198},{7,199},{8... | collective-permute-start | bytes 1572872 | tf_op jit(solution)/shard_map/ppermute | solution.py:37
  10.3 1.3 %collective-permute-start.9 = (f32[384,128]{1,0:T(8,128)S(1)}, f32[384,128]{1,0:T(8,128)}, u32[]{:S(2)}, u32[]{:S(2)}) collective-permute-start(f32[384,128]{1,0:T(8,128)S(1)} %add_add_fusion.6), channel_id=1, source_target_pairs={{0,6},{1,7},{16,22},{17,23},{64,70},{65,71},{80,86},{81,87},{128,1... | collective-permute-start | bytes 589832 | tf_op jit(solution)/shard_map/ppermute | solution.py:37
  11.7 21.3 %collective-permute-done.9 = f32[384,128]{1,0:T(8,128)} collective-permute-done((f32[384,128]{1,0:T(8,128)S(1)}, f32[384,128]{1,0:T(8,128)}, u32[]{:S(2)}, u32[]{:S(2)}) %collective-permute-start.9) | collective-permute-done | bytes 196640 | tf_op jit(solution)/shard_map/ppermute | solution.py:37
  33.0 1.0 add_add_fusion.5
  33.9 1.3 %collective-permute-start.12 = (f32[384,128]{1,0:T(8,128)S(1)}, f32[384,128]{1,0:T(8,128)S(1)}, u32[]{:S(2)}, u32[]{:S(2)}) collective-permute-start(f32[384,128]{1,0:T(8,128)S(1)} %add_add_fusion.5), channel_id=1, source_target_pairs={{0,14},{1,15},{6,4},{7,5},{16,30},{17,31},{22,20},{23,21},{64,78},... | collective-permute-start | bytes 589832 | tf_op jit(solution)/shard_map/ppermute | solution.py:37
  35.2 1.3 %collective-permute-start.11 = (f32[384,128]{1,0:T(8,128)S(1)}, f32[384,128]{1,0:T(8,128)S(1)}, u32[]{:S(2)}, u32[]{:S(2)}) collective-permute-start(f32[384,128]{1,0:T(8,128)S(1)} %add_add_fusion.5), channel_id=1, source_target_pairs={{0,2},{1,3},{6,8},{7,9},{10,12},{11,13},{16,18},{17,19},{22,24},{2... | collective-permute-start | bytes 589832 | tf_op jit(solution)/shard_map/ppermute | solution.py:37
  36.6 1.3 %add_add_fusion.3 = f32[256,512]{1,0:T(8,128)S(1)} fusion(f32[256,512]{1,0:T(8,128)} %collective-permute-done.2, f32[256,512]{1,0:T(8,128)S(1)} %select_select_fusion, f32[256,512]{1,0:T(8,128)} %collective-permute-done.1), kind=kLoop, calls=%fused_computation.3 | loop fusion | flops 262144 | bytes 2097152 | tf_op jit(solution)/shard_map/add | solution.py:63
  37.9 1.8 %collective-permute-done.11 = f32[384,128]{1,0:T(8,128)S(1)} collective-permute-done((f32[384,128]{1,0:T(8,128)S(1)}, f32[384,128]{1,0:T(8,128)S(1)}, u32[]{:S(2)}, u32[]{:S(2)}) %collective-permute-start.11) | collective-permute-done | bytes 196640 | tf_op jit(solution)/shard_map/ppermute | solution.py:37
  39.7 3.4 %collective-permute-start.17 = (f32[384,128]{1,0:T(8,128)S(1)}, f32[384,128]{1,0:T(8,128)S(1)}, u32[]{:S(2)}, u32[]{:S(2)}) collective-permute-start(f32[384,128]{1,0:T(8,128)S(1)} %add_add_fusion.4), channel_id=1, source_target_pairs={{0,16},{1,17},{2,18},{3,19},{4,20},{5,21},{6,22},{7,23},{8,24},{9,... | collective-permute-start | bytes 589832 | tf_op jit(solution)/shard_map/ppermute | solution.py:37
  43.2 1.3 %collective-permute-start.16 = (f32[384,128]{1,0:T(8,128)S(1)}, f32[384,128]{1,0:T(8,128)S(1)}, u32[]{:S(2)}, u32[]{:S(2)}) collective-permute-start(f32[384,128]{1,0:T(8,128)S(1)} %add_add_fusion.4), channel_id=1, source_target_pairs={{0,32},{1,33},{2,34},{3,35},{4,36},{5,37},{6,38},{7,39},{8,40},{9,... | collective-permute-start | bytes 589832 | tf_op jit(solution)/shard_map/ppermute | solution.py:37
  44.5 1.3 %collective-permute-start.15 = (f32[384,128]{1,0:T(8,128)S(1)}, f32[384,128]{1,0:T(8,128)S(1)}, u32[]{:S(2)}, u32[]{:S(2)}) collective-permute-start(f32[384,128]{1,0:T(8,128)S(1)} %add_add_fusion.4), channel_id=1, source_target_pairs={{0,48},{1,49},{2,50},{3,51},{4,52},{5,53},{6,54},{7,55},{8,56},{9,... | collective-permute-start | bytes 589832 | tf_op jit(solution)/shard_map/ppermute | solution.py:37
  46.5 1.3 %collective-permute-start.13 = (f32[512,256]{1,0:T(8,128)S(1)}, f32[512,256]{1,0:T(8,128)S(1)}, u32[]{:S(2)}, u32[]{:S(2)}) collective-permute-start(f32[512,256]{1,0:T(8,128)S(1)} %broadcast_select_fusion), channel_id=1, source_target_pairs={{0,6},{1,7},{16,22},{17,23},{32,38},{33,39},{48,54},{49,55},{64,70... | collective-permute-start | bytes 1572872 | tf_op jit(solution)/shard_map/ppermute | solution.py:37
  48.6 1.3 %collective-permute-start.3 = (f32[256,512]{1,0:T(8,128)S(1)}, f32[256,512]{1,0:T(8,128)S(1)}, u32[]{:S(2)}, u32[]{:S(2)}) collective-permute-start(f32[256,512]{1,0:T(8,128)S(1)} %add_add_fusion.3), channel_id=1, source_target_pairs={{0,64},{1,65},{2,66},{3,67},{4,68},{5,69},{6,70},{7,71},{8,72},{9,... | collective-permute-start | bytes 1572872 | tf_op jit(solution)/shard_map/ppermute | solution.py:37
  49.9 0.7 collective-permute-done.15
  50.7 1.9 %collective-permute-start.21 = (f32[640,128]{1,0:T(8,128)S(1)}, f32[640,128]{1,0:T(8,128)S(1)}, u32[]{:S(2)}, u32[]{:S(2)}) collective-permute-start(f32[640,128]{1,0:T(8,128)S(1)} %pad_maximum_fusion.own), channel_id=1, source_target_pairs={{0,1},{1,0},{2,3},{3,2},{4,5},{5,4},{6,7},{7,6},{8,9},{9,8},{10,11... | collective-permute-start | bytes 983048 | tf_op jit(solution)/shard_map/ppermute | solution.py:37
  52.7 8.0 %collective-permute-done.13 = f32[512,256]{1,0:T(8,128)S(1)} collective-permute-done((f32[512,256]{1,0:T(8,128)S(1)}, f32[512,256]{1,0:T(8,128)S(1)}, u32[]{:S(2)}, u32[]{:S(2)}) %collective-permute-start.13) | collective-permute-done | bytes 524320 | tf_op jit(solution)/shard_map/ppermute | solution.py:37
  60.8 3.7 %collective-permute-done.3 = f32[256,512]{1,0:T(8,128)S(1)} collective-permute-done((f32[256,512]{1,0:T(8,128)S(1)}, f32[256,512]{1,0:T(8,128)S(1)}, u32[]{:S(2)}, u32[]{:S(2)}) %collective-permute-start.3) | collective-permute-done | bytes 524320 | tf_op jit(solution)/shard_map/ppermute | solution.py:37
  64.6 2.2 %collective-permute-start.20 = (f32[512,256]{1,0:T(8,128)S(1)}, f32[512,256]{1,0:T(8,128)S(1)}, u32[]{:S(2)}, u32[]{:S(2)}) collective-permute-start(f32[512,256]{1,0:T(8,128)S(1)} %add_add_fusion.1), channel_id=1, source_target_pairs={{0,14},{1,15},{6,4},{7,5},{16,30},{17,31},{22,20},{23,21},{32,46},... | collective-permute-start | bytes 1572872 | tf_op jit(solution)/shard_map/ppermute | solution.py:37
  66.8 3.2 %collective-permute-start.19 = (f32[512,256]{1,0:T(8,128)S(1)}, f32[512,256]{1,0:T(8,128)S(1)}, u32[]{:S(2)}, u32[]{:S(2)}) collective-permute-start(f32[512,256]{1,0:T(8,128)S(1)} %add_add_fusion.1), channel_id=1, source_target_pairs={{0,2},{1,3},{6,8},{7,9},{10,12},{11,13},{16,18},{17,19},{22,24},{2... | collective-permute-start | bytes 1572872 | tf_op jit(solution)/shard_map/ppermute | solution.py:37
  70.1 4.9 %collective-permute-start.23 = (f32[256,512]{1,0:T(8,128)S(1)}, f32[256,512]{1,0:T(8,128)S(1)}, u32[]{:S(2)}, u32[]{:S(2)}) collective-permute-start(f32[256,512]{1,0:T(8,128)S(1)} %add_add_fusion.2.here), channel_id=1, source_target_pairs={{0,48},{1,49},{2,50},{3,51},{4,52},{5,53},{6,54},{7,55},{8,56},{9,... | collective-permute-start | bytes 1572872 | tf_op jit(solution)/shard_map/ppermute | solution.py:37
  75.0 2.3 %collective-permute-start.18 = (f32[256,512]{1,0:T(8,128)S(1)}, f32[256,512]{1,0:T(8,128)S(1)}, u32[]{:S(2)}, u32[]{:S(2)}) collective-permute-start(f32[256,512]{1,0:T(8,128)S(1)} %add_add_fusion.2.here), channel_id=1, source_target_pairs={{0,16},{1,17},{2,18},{3,19},{4,20},{5,21},{6,22},{7,23},{8,24},{9,... | collective-permute-start | bytes 1572872 | tf_op jit(solution)/shard_map/ppermute | solution.py:37
  77.3 9.1 %shard_map.17 = (f32[512,512]{1,0:T(8,128)S(1)}, f32[512,512]{1,0:T(8,128)S(1)}, f32[512,512]{1,0:T(8,128)S(1)}) custom-call(s32[4]{0:T(128)S(1)} %pad_add_fusion.place, f32[640,128]{1,0:T(8,128)S(1)} %pad_maximum_fusion.own, f32[640,128]{1,0:T(8,128)S(1)} %collective-permute-done.21.other), custom_call_target="tpu_custom_call" | custom-call | flops 3000000000 | bytes 1048576 | tf_op jit(solution)/shard_map/pallas_call | solution.py:341
  86.6 1.9 %collective-permute-start.22 = (f32[512,256]{1,0:T(8,128)S(1)}, f32[512,256]{1,0:T(8,128)S(1)}, u32[]{:S(2)}, u32[]{:S(2)}) collective-permute-start(f32[512,256]{1,0:T(8,128)S(1)} %add_add_fusion.own), channel_id=1, source_target_pairs={{0,1},{1,0},{2,3},{3,2},{4,5},{5,4},{6,7},{7,6},{8,9},{9,8},{10,11... | collective-permute-start | bytes 1572872 | tf_op jit(solution)/shard_map/ppermute | solution.py:37
  88.5 2.7 %collective-permute-start.24 = (f32[256,512]{1,0:T(8,128)S(1)}, f32[256,512]{1,0:T(8,128)S(1)}, u32[]{:S(2)}, u32[]{:S(2)}) collective-permute-start(f32[256,512]{1,0:T(8,128)S(1)} %collective-permute-done.18.beside), channel_id=1, source_target_pairs={{0,48},{1,49},{2,50},{3,51},{4,52},{5,53},{6,54},{7,55},{8,56},{9,... | collective-permute-start | bytes 1572872 | tf_op jit(solution)/shard_map/ppermute | solution.py:37
  91.2 4.4 %shard_map.18 = (f32[512,512]{1,0:T(8,128)S(1)}, f32[512,512]{1,0:T(8,128)S(1)}, f32[512,512]{1,0:T(8,128)S(1)}) custom-call(f32[512,512]{1,0:T(8,128)S(1)} %get-tuple-element.38.low_in, f32[512,512]{1,0:T(8,128)S(1)} %get-tuple-element.39.inv_in, f32[512,512]{1,0:T(8,128)S(1)} %get-tuple-element.40.a_in), custom_call_target="tpu_custom_call" | custom-call | flops 1500000000 | bytes 1048576 | tf_op jit(solution)/shard_map/pallas_call | solution.py:341
  95.6 5.6 %shard_map.19 = (f32[512,512]{1,0:T(8,128)S(1)}, f32[512,512]{1,0:T(8,128)S(1)}, f32[512,512]{1,0:T(8,128)S(1)}) custom-call(s32[4]{0:T(128)S(1)} %pad_add_fusion.place, f32[512,256]{1,0:T(8,128)S(1)} %add_add_fusion.own, f32[512,256]{1,0:T(8,128)S(1)} %collective-permute-done.22.other, f32[512,512]{1,0:T(8,128)S(1)} %get-tuple-element.41.low_in, ...), custom_call_target="tpu_custom_call" | custom-call | flops 1500000000 | bytes 1048576 | tf_op jit(solution)/shard_map/pallas_call | solution.py:341
  101.2 4.7 %collective-permute-done.24.opposite = f32[256,512]{1,0:T(8,128)S(1)} collective-permute-done((f32[256,512]{1,0:T(8,128)S(1)}, f32[256,512]{1,0:T(8,128)S(1)}, u32[]{:S(2)}, u32[]{:S(2)}) %collective-permute-start.24) | collective-permute-done | bytes 524320 | tf_op jit(solution)/shard_map/ppermute | solution.py:37
  105.9 3.9 %shard_map.20 = f32[512,1024]{1,0:T(8,128)} custom-call(s32[4]{0:T(128)S(1)} %pad_add_fusion.place, f32[512,1024]{1,0:T(8,128)S(1)} %copy-done, f32[512,512]{1,0:T(8,128)S(1)} %get-tuple-element.44.left, f32[512,512]{1,0:T(8,128)S(1)} %get-tuple-element.45.solved, f32[512,512]{1,0:T(8,128)S(1)} %get-tuple-element.46.low, f32[256,512]{1,0:T(8,128)S(1)} %add_add_fusion.2.here, ...), custom_call_target="tpu_custom_call" | custom-call | flops 1610612736 | bytes 6291456 | tf_op jit(solution)/shard_map/pallas_call | solution.py:357
  (42 shorter events, 5.8 us)
Async XLA Ops:
  0.0 6.5 %copy-start = (f32[512,1024]{1,0:T(8,128)S(1)}, f32[512,1024]{1,0:T(8,128)}, u32[]{:S(2)}) copy-start(f32[512,1024]{1,0:T(8,128)} %a.1) | copy-start | bytes 6291460
  1.2 5.3 %collective-permute-start = (f32[256,512]{1,0:T(8,128)S(1)}, f32[256,512]{1,0:T(8,128)}, u32[]{:S(2)}, u32[]{:S(2)}) collective-permute-start(f32[256,512]{1,0:T(8,128)S(1)} %slice.26), channel_id=1, source_target_pairs={{0,48},{1,49},{2,50},{3,51},{4,52},{5,53},{6,54},{7,55},{8,56},{9,... | collective-permute-start | bytes 1572872 | tf_op jit(solution)/shard_map/ppermute | solution.py:37
  3.7 1.4 %collective-permute-start.6 = (f32[384,128]{1,0:T(8,128)S(1)}, f32[384,128]{1,0:T(8,128)S(1)}, u32[]{:S(2)}, u32[]{:S(2)}) collective-permute-start(f32[384,128]{1,0:T(8,128)S(1)} %maximum_select_fusion), channel_id=1, source_target_pairs={{0,320},{1,321},{16,336},{17,337}} | collective-permute-start | bytes 589832 | tf_op jit(solution)/shard_map/ppermute | solution.py:37
  4.4 0.7 collective-permute-start.5
  5.1 4.5 %collective-permute-start.8 = (f32[384,128]{1,0:T(8,128)S(1)}, f32[384,128]{1,0:T(8,128)S(1)}, u32[]{:S(2)}, u32[]{:S(2)}) collective-permute-start(f32[384,128]{1,0:T(8,128)S(1)} %add_add_fusion.7), channel_id=1, source_target_pairs={{0,448},{1,449},{16,464},{17,465},{192,128},{193,129},{208,144},{2... | collective-permute-start | bytes 589832 | tf_op jit(solution)/shard_map/ppermute | solution.py:37
  5.8 3.8 %collective-permute-start.7 = (f32[384,128]{1,0:T(8,128)S(1)}, f32[384,128]{1,0:T(8,128)S(1)}, u32[]{:S(2)}, u32[]{:S(2)}) collective-permute-start(f32[384,128]{1,0:T(8,128)S(1)} %add_add_fusion.7), channel_id=1, source_target_pairs={{0,64},{1,65},{16,80},{17,81},{192,256},{193,257},{208,272},{209,2... | collective-permute-start | bytes 589832 | tf_op jit(solution)/shard_map/ppermute | solution.py:37
  6.6 29.9 %collective-permute-start.2 = (f32[256,512]{1,0:T(8,128)S(1)}, f32[256,512]{1,0:T(8,128)}, u32[]{:S(2)}, u32[]{:S(2)}) collective-permute-start(f32[256,512]{1,0:T(8,128)S(1)} %select_select_fusion), channel_id=1, source_target_pairs={{0,320},{1,321},{2,322},{3,323},{4,324},{5,325},{6,326},{7,327},{8... | collective-permute-start | bytes 1572872 | tf_op jit(solution)/shard_map/ppermute | solution.py:37
  8.1 28.5 %collective-permute-start.1 = (f32[256,512]{1,0:T(8,128)S(1)}, f32[256,512]{1,0:T(8,128)}, u32[]{:S(2)}, u32[]{:S(2)}) collective-permute-start(f32[256,512]{1,0:T(8,128)S(1)} %select_select_fusion), channel_id=1, source_target_pairs={{0,192},{1,193},{2,194},{3,195},{4,196},{5,197},{6,198},{7,199},{8... | collective-permute-start | bytes 1572872 | tf_op jit(solution)/shard_map/ppermute | solution.py:37
  9.6 2.1 %collective-permute-start.10 = (f32[384,128]{1,0:T(8,128)S(1)}, f32[384,128]{1,0:T(8,128)S(1)}, u32[]{:S(2)}, u32[]{:S(2)}) collective-permute-start(f32[384,128]{1,0:T(8,128)S(1)} %add_add_fusion.6), channel_id=1, source_target_pairs={{0,10},{1,11},{16,26},{17,27},{64,74},{65,75},{80,90},{81,91},{128... | collective-permute-start | bytes 589832 | tf_op jit(solution)/shard_map/ppermute | solution.py:37
  10.3 22.7 %collective-permute-start.9 = (f32[384,128]{1,0:T(8,128)S(1)}, f32[384,128]{1,0:T(8,128)}, u32[]{:S(2)}, u32[]{:S(2)}) collective-permute-start(f32[384,128]{1,0:T(8,128)S(1)} %add_add_fusion.6), channel_id=1, source_target_pairs={{0,6},{1,7},{16,22},{17,23},{64,70},{65,71},{80,86},{81,87},{128,1... | collective-permute-start | bytes 589832 | tf_op jit(solution)/shard_map/ppermute | solution.py:37
  33.9 5.8 %collective-permute-start.12 = (f32[384,128]{1,0:T(8,128)S(1)}, f32[384,128]{1,0:T(8,128)S(1)}, u32[]{:S(2)}, u32[]{:S(2)}) collective-permute-start(f32[384,128]{1,0:T(8,128)S(1)} %add_add_fusion.5), channel_id=1, source_target_pairs={{0,14},{1,15},{6,4},{7,5},{16,30},{17,31},{22,20},{23,21},{64,78},... | collective-permute-start | bytes 589832 | tf_op jit(solution)/shard_map/ppermute | solution.py:37
  35.2 4.5 %collective-permute-start.11 = (f32[384,128]{1,0:T(8,128)S(1)}, f32[384,128]{1,0:T(8,128)S(1)}, u32[]{:S(2)}, u32[]{:S(2)}) collective-permute-start(f32[384,128]{1,0:T(8,128)S(1)} %add_add_fusion.5), channel_id=1, source_target_pairs={{0,2},{1,3},{6,8},{7,9},{10,12},{11,13},{16,18},{17,19},{22,24},{2... | collective-permute-start | bytes 589832 | tf_op jit(solution)/shard_map/ppermute | solution.py:37
  39.7 8.1 %collective-permute-start.17 = (f32[384,128]{1,0:T(8,128)S(1)}, f32[384,128]{1,0:T(8,128)S(1)}, u32[]{:S(2)}, u32[]{:S(2)}) collective-permute-start(f32[384,128]{1,0:T(8,128)S(1)} %add_add_fusion.4), channel_id=1, source_target_pairs={{0,16},{1,17},{2,18},{3,19},{4,20},{5,21},{6,22},{7,23},{8,24},{9,... | collective-permute-start | bytes 589832 | tf_op jit(solution)/shard_map/ppermute | solution.py:37
  43.2 5.5 %collective-permute-start.16 = (f32[384,128]{1,0:T(8,128)S(1)}, f32[384,128]{1,0:T(8,128)S(1)}, u32[]{:S(2)}, u32[]{:S(2)}) collective-permute-start(f32[384,128]{1,0:T(8,128)S(1)} %add_add_fusion.4), channel_id=1, source_target_pairs={{0,32},{1,33},{2,34},{3,35},{4,36},{5,37},{6,38},{7,39},{8,40},{9,... | collective-permute-start | bytes 589832 | tf_op jit(solution)/shard_map/ppermute | solution.py:37
  44.5 6.2 %collective-permute-start.15 = (f32[384,128]{1,0:T(8,128)S(1)}, f32[384,128]{1,0:T(8,128)S(1)}, u32[]{:S(2)}, u32[]{:S(2)}) collective-permute-start(f32[384,128]{1,0:T(8,128)S(1)} %add_add_fusion.4), channel_id=1, source_target_pairs={{0,48},{1,49},{2,50},{3,51},{4,52},{5,53},{6,54},{7,55},{8,56},{9,... | collective-permute-start | bytes 589832 | tf_op jit(solution)/shard_map/ppermute | solution.py:37
  45.8 6.9 %collective-permute-start.14 = (f32[512,256]{1,0:T(8,128)S(1)}, f32[512,256]{1,0:T(8,128)S(1)}, u32[]{:S(2)}, u32[]{:S(2)}) collective-permute-start(f32[512,256]{1,0:T(8,128)S(1)} %broadcast_select_fusion), channel_id=1, source_target_pairs={{0,10},{1,11},{16,26},{17,27},{32,42},{33,43},{48,58},{49,59},{64,... | collective-permute-start | bytes 1572872 | tf_op jit(solution)/shard_map/ppermute | solution.py:37
  46.5 14.1 %collective-permute-start.13 = (f32[512,256]{1,0:T(8,128)S(1)}, f32[512,256]{1,0:T(8,128)S(1)}, u32[]{:S(2)}, u32[]{:S(2)}) collective-permute-start(f32[512,256]{1,0:T(8,128)S(1)} %broadcast_select_fusion), channel_id=1, source_target_pairs={{0,6},{1,7},{16,22},{17,23},{32,38},{33,39},{48,54},{49,55},{64,70... | collective-permute-start | bytes 1572872 | tf_op jit(solution)/shard_map/ppermute | solution.py:37
  47.8 12.9 %collective-permute-start.4 = (f32[256,512]{1,0:T(8,128)S(1)}, f32[256,512]{1,0:T(8,128)S(1)}, u32[]{:S(2)}, u32[]{:S(2)}) collective-permute-start(f32[256,512]{1,0:T(8,128)S(1)} %add_add_fusion.3), channel_id=1, source_target_pairs={{0,448},{1,449},{2,450},{3,451},{4,452},{5,453},{6,454},{7,455},{8... | collective-permute-start | bytes 1572872 | tf_op jit(solution)/shard_map/ppermute | solution.py:37
  48.6 15.8 %collective-permute-start.3 = (f32[256,512]{1,0:T(8,128)S(1)}, f32[256,512]{1,0:T(8,128)S(1)}, u32[]{:S(2)}, u32[]{:S(2)}) collective-permute-start(f32[256,512]{1,0:T(8,128)S(1)} %add_add_fusion.3), channel_id=1, source_target_pairs={{0,64},{1,65},{2,66},{3,67},{4,68},{5,69},{6,70},{7,71},{8,72},{9,... | collective-permute-start | bytes 1572872 | tf_op jit(solution)/shard_map/ppermute | solution.py:37
  50.7 26.6 %collective-permute-start.21 = (f32[640,128]{1,0:T(8,128)S(1)}, f32[640,128]{1,0:T(8,128)S(1)}, u32[]{:S(2)}, u32[]{:S(2)}) collective-permute-start(f32[640,128]{1,0:T(8,128)S(1)} %pad_maximum_fusion.own), channel_id=1, source_target_pairs={{0,1},{1,0},{2,3},{3,2},{4,5},{5,4},{6,7},{7,6},{8,9},{9,8},{10,11... | collective-permute-start | bytes 983048 | tf_op jit(solution)/shard_map/ppermute | solution.py:37
  64.6 21.8 %collective-permute-start.20 = (f32[512,256]{1,0:T(8,128)S(1)}, f32[512,256]{1,0:T(8,128)S(1)}, u32[]{:S(2)}, u32[]{:S(2)}) collective-permute-start(f32[512,256]{1,0:T(8,128)S(1)} %add_add_fusion.1), channel_id=1, source_target_pairs={{0,14},{1,15},{6,4},{7,5},{16,30},{17,31},{22,20},{23,21},{32,46},... | collective-permute-start | bytes 1572872 | tf_op jit(solution)/shard_map/ppermute | solution.py:37
  66.8 19.6 %collective-permute-start.19 = (f32[512,256]{1,0:T(8,128)S(1)}, f32[512,256]{1,0:T(8,128)S(1)}, u32[]{:S(2)}, u32[]{:S(2)}) collective-permute-start(f32[512,256]{1,0:T(8,128)S(1)} %add_add_fusion.1), channel_id=1, source_target_pairs={{0,2},{1,3},{6,8},{7,9},{10,12},{11,13},{16,18},{17,19},{22,24},{2... | collective-permute-start | bytes 1572872 | tf_op jit(solution)/shard_map/ppermute | solution.py:37
  70.1 21.1 %collective-permute-start.23 = (f32[256,512]{1,0:T(8,128)S(1)}, f32[256,512]{1,0:T(8,128)S(1)}, u32[]{:S(2)}, u32[]{:S(2)}) collective-permute-start(f32[256,512]{1,0:T(8,128)S(1)} %add_add_fusion.2.here), channel_id=1, source_target_pairs={{0,48},{1,49},{2,50},{3,51},{4,52},{5,53},{6,54},{7,55},{8,56},{9,... | collective-permute-start | bytes 1572872 | tf_op jit(solution)/shard_map/ppermute | solution.py:37
  75.0 11.5 %collective-permute-start.18 = (f32[256,512]{1,0:T(8,128)S(1)}, f32[256,512]{1,0:T(8,128)S(1)}, u32[]{:S(2)}, u32[]{:S(2)}) collective-permute-start(f32[256,512]{1,0:T(8,128)S(1)} %add_add_fusion.2.here), channel_id=1, source_target_pairs={{0,16},{1,17},{2,18},{3,19},{4,20},{5,21},{6,22},{7,23},{8,24},{9,... | collective-permute-start | bytes 1572872 | tf_op jit(solution)/shard_map/ppermute | solution.py:37
  86.6 9.1 %collective-permute-start.22 = (f32[512,256]{1,0:T(8,128)S(1)}, f32[512,256]{1,0:T(8,128)S(1)}, u32[]{:S(2)}, u32[]{:S(2)}) collective-permute-start(f32[512,256]{1,0:T(8,128)S(1)} %add_add_fusion.own), channel_id=1, source_target_pairs={{0,1},{1,0},{2,3},{3,2},{4,5},{5,4},{6,7},{7,6},{8,9},{9,8},{10,11... | collective-permute-start | bytes 1572872 | tf_op jit(solution)/shard_map/ppermute | solution.py:37
  88.5 17.4 %collective-permute-start.24 = (f32[256,512]{1,0:T(8,128)S(1)}, f32[256,512]{1,0:T(8,128)S(1)}, u32[]{:S(2)}, u32[]{:S(2)}) collective-permute-start(f32[256,512]{1,0:T(8,128)S(1)} %collective-permute-done.18.beside), channel_id=1, source_target_pairs={{0,48},{1,49},{2,50},{3,51},{4,52},{5,53},{6,54},{7,55},{8,56},{9,... | collective-permute-start | bytes 1572872 | tf_op jit(solution)/shard_map/ppermute | solution.py:37
